TPU v7x, 32 devices: a whole 2x2x4 slice. The times are simulated.
32 devices in a mesh: fsdp: 8 (over y, x, core), tensor: 4 (over z).
Axes of the slice: x: 2, y: 2, z: 4, core: 2. Of those that a mesh axis runs over, the one named last changes fastest.
Arguments:
- tokens: bfloat16 [2048, 2048], P('fsdp'), may hold values from -6 to 6
- cotangent: bfloat16 [2048, 2048], P('fsdp'), may hold values from -6 to 6
- routes: int32 [2048, 8], P('fsdp'), may hold values from 0 to 63, all different within a row; in each aligned block of 256 rows (0 to 255, 256 to 511, ...) at most 40 rows name the same one
- w_query: bfloat16 [2048, 2048], P('fsdp', 'tensor'), may hold values from -0.125 to 0.125
- w_key: bfloat16 [2048, 2048], P('fsdp', 'tensor'), may hold values from -0.125 to 0.125
- w_value: bfloat16 [2048, 2048], P('fsdp', 'tensor'), may hold values from -0.125 to 0.125
- w_output: bfloat16 [2048, 2048], P('fsdp', 'tensor'), may hold values from -1.25 to 1.25
- w_router: bfloat16 [2048, 64], P('fsdp'), may hold values from -0.0625 to 0.0625
- attn_gain: bfloat16 [2048], P('fsdp'), may hold values from 0.25 to 1.75
- ffn_gain: bfloat16 [2048], P('fsdp'), may hold values from 0.25 to 1.75
- query_gain: bfloat16 [128], P('fsdp'), may hold values from 0.25 to 1.75
- key_gain: bfloat16 [128], P('fsdp'), may hold values from 0.25 to 1.75
- expert_weights: bfloat16 [64, 3, 2048, 1024], P('fsdp', None, None, 'tensor'), may hold values from -4 to 4
Outputs:
- layer_out: bfloat16 [2048, 2048], P('fsdp')
- grad_tokens: bfloat16 [2048, 2048], P('fsdp')
- grad_query: float32 [2048, 2048], P('fsdp', 'tensor')
- grad_key: float32 [2048, 2048], P('fsdp', 'tensor')
- grad_value: float32 [2048, 2048], P('fsdp', 'tensor')
- grad_output: float32 [2048, 2048], P('fsdp', 'tensor')
- grad_router: float32 [2048, 64], P('fsdp')
- grad_attn_gain: float32 [2048], P('fsdp')
- grad_ffn_gain: float32 [2048], P('fsdp')
- grad_query_gain: float32 [128], P('fsdp')
- grad_key_gain: float32 [128], P('fsdp')
- grad_experts: float32 [64, 3, 2048, 1024], P('fsdp', None, None, 'tensor')
Inputs may be any that keep to these rules, and one draw needn't show every extreme that they name: `routes`: each row names 8 different experts. Among the 256 rows of one index of fsdp no expert is named more than 40 times, a bound that some expert reaches in some such block.
All inputs are finite; a program needn't handle non-finite values.
Results may differ from a plain program's by a relative error of at most 0.02.
Values may be sent and summed in bfloat16 or wider, within the bound.
No kernel may reach another device: no remote copies, remote signals or barrier semaphores. Data moves between devices by JAX's collectives and lax.ppermute only.
A program may use at most 320 MiB of HBM per device.

v0:
```python
import functools

import jax
import jax.numpy as jnp
from jax import lax
from jax.experimental import pallas as pl
from jax.experimental.pallas import tpu as pltpu
from jax.sharding import PartitionSpec as P

D = 2048
HD = 128
EXPERTS = 64
CAP = 40
SIDE = 128
EPSILON = 1e-06
ROPE_BASE = 10000.0

F32 = jnp.float32
BF16 = jnp.bfloat16
VMEM = pl.BlockSpec(memory_space=pltpu.VMEM)
SMEM = pl.BlockSpec(memory_space=pltpu.SMEM)
HBM = pl.BlockSpec(memory_space=pltpu.HBM)
MIB = 1024 * 1024


def shape(dims, dtype):
    return jax.ShapeDtypeStruct(tuple(dims), dtype)


def params(mebibytes=16):
    return pltpu.CompilerParams(vmem_limit_bytes=mebibytes * MIB)


def near_core(array):
    return pltpu.with_memory_space_constraint(array, pltpu.VMEM)


def cost(micros):
    return pl.CostEstimate(
        flops=int(micros * 1e9), bytes_accessed=int(micros * 3e6), transcendentals=0
    )


def in_hbm(arrays):
    return [pltpu.with_memory_space_constraint(array, pltpu.HBM) for array in arrays]


def dot(left, right):
    return jnp.dot(left, right, preferred_element_type=F32)


def dot_nt(left, right):
    return lax.dot_general(left, right, (((1,), (1,)), ((), ())), preferred_element_type=F32)


def dot_tn(left, right):
    return lax.dot_general(left, right, (((0,), (0,)), ((), ())), preferred_element_type=F32)


def rms_inverse(values):
    return lax.rsqrt(jnp.mean(values * values, axis=-1, keepdims=True) + EPSILON)


def norm_backward(values, inverse, gain, upstream):
    scaled = gain * upstream
    return inverse * scaled - values * (inverse * inverse * inverse) * jnp.mean(
        values * scaled, axis=-1, keepdims=True
    )


def half_turn(values):
    return pltpu.roll(values, HD // 2, 1)


def lanes(dims):
    return lax.broadcasted_iota(jnp.int32, dims, len(dims) - 1)


def swap(block, axis, size, step):
    return lax.ppermute(block, axis, [(i, i ^ step) for i in range(size)])


def without(kernel, at, number):
    def body(*refs):
        kernel(*refs[:at], *refs[at + number :])

    return body


def through(moves, buffer, sems):
    arriving, leaving, row = [], [], 0
    for k, (source, target) in enumerate(moves):
        here = buffer.at[pl.ds(row, source.shape[0]), :]
        arriving.append(pltpu.make_async_copy(source, here, sems.at[2 * k]))
        leaving.append(pltpu.make_async_copy(here, target, sems.at[2 * k + 1]))
        arriving[-1].start()
        row += source.shape[0]
    for arrives, leaves in zip(arriving, leaving):
        arrives.wait()
        leaves.start()
    for leaves in leaving:
        leaves.wait()


def joins(groups, deps=()):
    parts = [part for group in groups for part in group]
    count = len(parts)
    features, dtype = parts[0].shape[1], parts[0].dtype
    totals = [sum(part.shape[0] for part in group) for group in groups]

    def kernel(*refs):
        out_refs, (buffer, sems) = refs[count:-2], refs[-2:]
        moves, k = [], 0
        for out_ref, group in zip(out_refs, groups):
            row = 0
            for part in group:
                moves.append((refs[k], out_ref.at[pl.ds(row, part.shape[0]), :]))
                row, k = row + part.shape[0], k + 1
        through(moves, buffer, sems)

    return pl.pallas_call(
        without(kernel, count, len(deps)),
        out_shape=[shape((total, features), dtype) for total in totals],
        in_specs=[HBM] * (count + len(deps)),
        out_specs=[HBM] * len(groups),
        scratch_shapes=[
            pltpu.VMEM((sum(totals), features), dtype),
            pltpu.SemaphoreType.DMA((2 * count,)),
        ],
        compiler_params=params(60),
        cost_estimate=cost(0.1),
        name="joins",
    )(*parts, *deps)


def join(parts, deps=()):
    return joins([parts], deps)[0]


def relay(parts, deps):
    return joins([[part] for part in parts], deps)


def halves(upper_of, lower_of, deps=()):
    rows, features = upper_of.shape
    half = rows // 2

    def kernel(upper_ref, lower_ref, upper_out, lower_out, buffer, sems):
        through(
            [
                (upper_ref.at[pl.ds(0, half), :], upper_out),
                (lower_ref.at[pl.ds(half, half), :], lower_out),
            ],
            buffer,
            sems,
        )

    return pl.pallas_call(
        without(kernel, 2, len(deps)),
        out_shape=[shape((half, features), upper_of.dtype)] * 2,
        in_specs=[HBM] * (2 + len(deps)),
        out_specs=[HBM] * 2,
        scratch_shapes=[
            pltpu.VMEM((rows, features), upper_of.dtype),
            pltpu.SemaphoreType.DMA((4,)),
        ],
        compiler_params=params(),
        cost_estimate=cost(0.1),
        name="halves",
    )(upper_of, lower_of, *deps)


def gather_near(block, size):
    if size != 8:
        return [swap(block, "fsdp", size, p) for p in range(1, size)]
    return [swap(block, "fsdp", size, 2), swap(block, "fsdp", size, 4)]


def gather_rest(block, near, size, deps=()):
    rows = block.shape[0]
    if size != 8:
        return [(p, 0, part, 0, rows) for p, part in enumerate([block] + near)]
    half = rows // 2
    upper, lower = halves(near[1], near[0], deps)
    front = swap(upper, "fsdp", size, 2)
    back = swap(lower, "fsdp", size, 4)
    pieces = []
    for k, part in enumerate([block] + near):
        pieces.append((2 * k, 0, part, 0, rows))
        pieces.append((2 * k + 1, 0, swap(part, "fsdp", size, 1), 0, rows))
    for row, part in ((0, front), (half, back)):
        pieces.append((6, row, part, 0, half))
        pieces.append((7, row, swap(part, "fsdp", size, 1), 0, half))
    return pieces


def gather_two(blocks, near, size, sources=None):
    pieces = []
    start = 0
    sources = sources or [near[0][1], near[1][0]]
    for block, (along_x, along_y), source, step in zip(blocks, near, sources, (2, 4)):
        rows = block.shape[0]
        last = swap(source, "fsdp", size, step)
        for index, part in ((0, block), (2, along_x), (4, along_y), (6, last)):
            pieces.append((index, start, part, 0, rows))
            pieces.append((index + 1, start, swap(part, "fsdp", size, 1), 0, rows))
        start += rows
    return pieces


def arrays_of(pieces):
    found = []
    for _, _, part, _, _ in pieces:
        if not any(part is other for other in found):
            found.append(part)
    return found


def start_fetch(pieces, refs, place, sems, own=None):
    arrays = arrays_of(pieces)
    copies = []
    for k, (index, row, part, at, rows) in enumerate(pieces):
        ref = next(ref for other, ref in zip(arrays, refs) if other is part)
        if at is None:
            at = pl.multiple_of((own ^ index) * rows, 16)
        copy = pltpu.make_async_copy(
            ref.at[pl.ds(at, rows), :], place(index, row, rows), sems.at[k]
        )
        copy.start()
        copies.append(copy)
    return copies


def pair_sums(keep, got, deps=()):
    _, rows, columns = keep.shape
    half = rows // 2

    def kernel(keep_ref, got_ref, out_x, out_y, held, sems):
        upper, lower = pl.ds(0, half), pl.ds(half, half)
        places = [(1, upper), (3, upper), (2, lower), (3, lower)]
        copies = fetch_parts([keep_ref.at[place] for place in places], held, sems)
        for k, place in enumerate(places):
            copies[k].wait()
            (out_x, out_y)[k // 2][k % 2] = (
                held[k].astype(F32) + got_ref[place].astype(F32)
            ).astype(BF16)

    return pl.pallas_call(
        without(kernel, 2, len(deps)),
        out_shape=[shape((2, half, columns), BF16)] * 2,
        in_specs=[HBM, VMEM] + [HBM] * len(deps),
        out_specs=[VMEM] * 2,
        scratch_shapes=[pltpu.VMEM((4, half, columns), BF16), pltpu.SemaphoreType.DMA((4,))],
        compiler_params=params(),
        cost_estimate=cost(0.1),
        name="pair_sums",
    )(*in_hbm([keep]), near_core(got), *in_hbm(deps))


def fetch_parts(parts, buffer, sems):
    copies = []
    for k, part in enumerate(parts):
        copies.append(pltpu.make_async_copy(part, buffer.at[k], sems.at[k]))
        copies[-1].start()
    return copies


def next_sums(keep, got, from_x, from_y, deps, micros):
    _, rows, columns = keep.shape
    half = rows // 2

    def kernel(keep_ref, got_ref, new_x, new_y, out_x, out_y, held, sems):
        upper, lower = pl.ds(0, half), pl.ds(half, half)
        places = [(2, upper), (1, lower)]
        copies = fetch_parts([keep_ref.at[place] for place in places], held, sems)
        for k, (new, out) in enumerate(((new_x, out_x), (new_y, out_y))):
            copies[k].wait()
            out[...] = (
                held[k].astype(F32) + got_ref[places[k]].astype(F32) + new[1].astype(F32)
            ).astype(BF16)

    return pl.pallas_call(
        without(kernel, 4, len(deps)),
        out_shape=[shape((half, columns), BF16)] * 2,
        in_specs=[HBM, VMEM, VMEM, VMEM] + [HBM] * len(deps),
        out_specs=[VMEM] * 2,
        scratch_shapes=[pltpu.VMEM((2, half, columns), BF16), pltpu.SemaphoreType.DMA((2,))],
        compiler_params=params(),
        cost_estimate=cost(micros),
        name="next_sums",
    )(*in_hbm([keep]), near_core(got), near_core(from_x), near_core(from_y), *in_hbm(deps))


def last_sums(keep, got, from_x, from_y, last_x, last_y, count, deps=()):
    _, rows, columns = keep.shape
    half = rows // 2
    part = rows // count
    each = half // part

    def kernel(keep_ref, got_ref, new_x, end_x, new_y, end_y, *refs):
        out_refs, (held, sems) = refs[:count], refs[count:]
        upper, lower = pl.ds(0, half), pl.ds(half, half)
        places = [(0, upper), (0, lower)]
        copies = fetch_parts([keep_ref.at[place] for place in places], held, sems)
        for k in range(count):
            side = k // each
            new, end = (new_x, end_x) if side == 0 else (new_y, end_y)
            if k % each == 0:
                copies[side].wait()
            first = (k % each) * part
            span = slice(first, first + part)
            from_got = slice(side * half + first, side * half + first + part)
            total = held[side, span].astype(F32) + got_ref[0, from_got].astype(F32)
            total = total + new[0, span].astype(F32) + end[span].astype(F32)
            out_refs[k][...] = total.astype(BF16)

    return pl.pallas_call(
        without(kernel, 6, len(deps)),
        out_shape=[shape((part, columns), BF16)] * count,
        in_specs=[HBM] + [VMEM] * 5 + [HBM] * len(deps),
        out_specs=[VMEM] * count,
        scratch_shapes=[pltpu.VMEM((2, half, columns), BF16), pltpu.SemaphoreType.DMA((2,))],
        compiler_params=params(),
        cost_estimate=cost(20),
        name="last_sums",
    )(
        *in_hbm([keep]), near_core(got), near_core(from_x), near_core(last_x), near_core(from_y), near_core(last_y),
        *in_hbm(deps),
    )


def column_sums(keep, got, from_x, from_y, last_x, last_y, widths, turned):
    _, rows, columns = keep.shape
    half = rows // 2

    def kernel(keep_x, got_x, new_x, end_x, keep_y, got_y, new_y, end_y, *out_refs):
        for k, refs in enumerate(((keep_x, got_x, new_x, end_x), (keep_y, got_y, new_y, end_y))):
            span = slice(k * half, (k + 1) * half)
            total = refs[0][0].astype(F32)
            for ref in refs[1:3]:
                total = total + ref[0].astype(F32)
            total = total + refs[3][...].astype(F32)
            column = 0
            for width, out_ref in zip(widths, out_refs):
                out_ref[span, :] = total[:, column : column + width]
                column += width
            if turned:
                out_refs[-1][:, span] = jnp.transpose(total[:, column : column + turned])

    block = (1, half, columns)
    first = pl.BlockSpec(block, lambda j: (0, 0, 0))
    second = pl.BlockSpec(block, lambda j: (0, 1, 0))
    end = pl.BlockSpec((half, columns), lambda j: (0, 0))
    shapes = [(rows, width) for width in widths] + [(turned, rows)] * (turned > 0)
    return pl.pallas_call(
        kernel,
        out_shape=[shape(dims, F32) for dims in shapes],
        grid=(1,),
        in_specs=[first, first, first, end, second, second, first, end],
        out_specs=[pl.BlockSpec(dims, lambda j: (0, 0)) for dims in shapes],
        compiler_params=params(),
        cost_estimate=cost(0.1),
        name="column_sums",
    )(keep, got, from_x, last_x, keep, got, from_y, last_y)


def halve(array, deps=()):
    rows, columns = array.shape
    half = columns // 2

    def kernel(ref, left_ref, right_ref):
        left_ref[...] = ref[:, :half]
        right_ref[...] = ref[:, half:]

    return pl.pallas_call(
        without(kernel, 1, len(deps)),
        out_shape=[shape((rows, half), array.dtype)] * 2,
        grid=(2,),
        in_specs=[pl.BlockSpec((rows // 2, columns), lambda j: (j, 0))] + [HBM] * len(deps),
        out_specs=[pl.BlockSpec((rows // 2, half), lambda j: (j, 0))] * 2,
        compiler_params=params(60),
        cost_estimate=cost(0.1),
        name="halve",
    )(array, *deps)


class Reduce:
    def __init__(self, keep, send, size):
        self.keep, self.send, self.size = keep, send, size
        if size == 8:
            self.got = swap(send, "fsdp", size, 1)

    def first(self, deps=()):
        if self.size != 8:
            return []
        self.pair = pair_sums(self.keep, self.got, deps)
        self.from_x = swap(self.pair[0], "fsdp", self.size, 2)
        self.from_y = swap(self.pair[1], "fsdp", self.size, 4)
        return list(self.pair[:1])

    def second(self, deps=(), micros=0.1):
        if self.size != 8:
            return []
        sums = next_sums(self.keep, self.got, self.from_x, self.from_y, deps, micros)
        self.last_x = swap(sums[0], "fsdp", self.size, 4)
        self.last_y = swap(sums[1], "fsdp", self.size, 2)
        return list(sums[:1])

    def total(self):
        if self.size != 8:
            total = self.keep[0].astype(F32)
            for p in range(1, self.size):
                block = self.keep[p // 2] if p % 2 == 0 else self.send[p // 2]
                total = total + swap(block, "fsdp", self.size, p).astype(F32)
            return total
        half = self.keep.shape[1] // 2
        sums = []
        for rows, new, last in (
            (slice(0, half), self.from_x, self.last_x),
            (slice(half, None), self.from_y, self.last_y),
        ):
            sums.append(
                self.keep[0, rows].astype(F32)
                + self.got[0, rows].astype(F32)
                + new[0].astype(F32)
                + last.astype(F32)
            )
        return jnp.concatenate(sums, axis=0)

    def columns(self, widths, turned=0):
        if self.size == 8:
            return column_sums(
                self.keep, self.got, self.from_x, self.from_y, self.last_x, self.last_y, widths, turned
            )
        total, found, column = self.total(), [], 0
        for width in widths:
            found.append(total[:, column : column + width])
            column += width
        return found + [total[:, column : column + turned].T] * (turned > 0)

    def rows(self, count, deps=()):
        if self.size != 8:
            return jnp.split(self.total().astype(BF16), count, axis=0)
        return last_sums(
            self.keep, self.got, self.from_x, self.from_y, self.last_x, self.last_y, count, deps
        )


def attend_forward(pos, tokens, cosine, sine, pieces, nf, nt, deps=()):
    length = tokens.shape[0]
    block = D // nf
    rows = length // nt
    columns = pieces[0][2].shape[1]
    width = (columns - SIDE) // 4
    heads = width // HD
    arrays = arrays_of(pieces)
    count = len(arrays)

    def kernel(pos_ref, x_ref, cos_ref, sin_ref, *refs):
        piece_refs, refs = refs[:count], refs[count:]
        n1_ref, qk_ref, rot_ref, v_ref, prob_ref, att_ref, side_ref, gain_ref, head_gain_ref = refs[:9]
        part_refs, (w, out, sems) = refs[9 : 9 + nt], refs[9 + nt :]
        f, t = pos_ref[0], pos_ref[1]

        def place(index, row, number):
            start = pl.multiple_of((f ^ index) * block + row, 16)
            return w.at[pl.ds(start, number), :]

        copies = start_fetch(pieces, piece_refs, place, sems)
        x = x_ref[...].astype(F32)
        normed = x * rms_inverse(x)
        for copy in copies:
            copy.wait()
        side_ref[...] = w[:, 4 * width :]
        turned = jnp.transpose(w[:, 4 * width :].astype(F32))
        gain_ref[...] = turned[EXPERTS : EXPERTS + 8]
        head_rows = turned[EXPERTS : EXPERTS + 8, :block]
        for p in range(1, nf):
            head_rows = head_rows + turned[EXPERTS : EXPERTS + 8, p * block : (p + 1) * block]
        head_gains = head_rows[:, :HD]
        head_gain_ref[...] = head_gains
        n1 = (normed * turned[EXPERTS : EXPERTS + 1]).astype(BF16)
        n1_ref[...] = n1
        raw = dot(n1, w[:, : 3 * width])
        qk_ref[...] = raw[:, : 2 * width]
        v_ref[...] = raw[:, 2 * width :].astype(BF16)
        cos, sin = cos_ref[...], sin_ref[...]
        for h in range(heads):
            span = slice(h * HD, (h + 1) * HD)
            turned_rows = []
            for which in range(2):
                values = raw[:, which * width + h * HD : which * width + (h + 1) * HD]
                scaled = values * rms_inverse(values) * head_gains[2 + which : 3 + which]
                low = (scaled * cos + half_turn(scaled) * sin).astype(BF16)
                rot_ref[:, which * width + h * HD : which * width + (h + 1) * HD] = low
                turned_rows.append(low)
            scores = dot_nt(turned_rows[0], turned_rows[1]) * (HD**-0.5)
            shifted = jnp.exp(scores - jnp.max(scores, axis=-1, keepdims=True))
            probs = shifted / jnp.sum(shifted, axis=-1, keepdims=True)
            prob_ref[h] = probs
            att_ref[:, span] = dot(probs.astype(BF16), v_ref[:, span]).astype(BF16)
        out[...] = dot_nt(att_ref[...], w[:, 3 * width : 4 * width]).astype(BF16)
        for d in range(nt):
            start = pl.multiple_of((t ^ d) * rows, 16)
            part_refs[d][...] = out[pl.ds(start, rows), :]

    results = pl.pallas_call(
        without(kernel, 4 + count, len(deps)),
        out_shape=[
            shape((length, D), BF16),
            shape((length, 2 * width), F32),
            shape((length, 2 * width), BF16),
            shape((length, width), BF16),
            shape((heads, length, length), F32),
            shape((length, width), BF16),
            shape((D, SIDE), BF16),
            shape((8, D), F32),
            shape((8, HD), F32),
        ]
        + [shape((rows, D), BF16)] * nt,
        in_specs=[SMEM, VMEM, VMEM, VMEM] + [HBM] * (count + len(deps)),
        out_specs=[VMEM] * (9 + nt),
        scratch_shapes=[
            pltpu.VMEM((D, columns), BF16),
            pltpu.VMEM((length, D), BF16),
            pltpu.SemaphoreType.DMA((len(pieces),)),
        ],
        compiler_params=params(60),
        cost_estimate=cost(5),
        name="attend_forward",
    )(pos, tokens, cosine, sine, *arrays, *deps)
    return results[:9], results[9:]


def attend_backward(pos, grad_rows, ffn_row, layer_sum, pieces, saved, tokens, cosine, sine, nf, nt, deps=()):
    _, qk, rot, values, probs, _, _, gains, head_gains = saved
    length = tokens.shape[0]
    block = D // nf
    rows = length // nt
    columns = pieces[0][2].shape[1]
    width = (columns - SIDE) // 4
    heads = width // HD
    more = gain_columns(rows)
    arrays = arrays_of(pieces)
    count = len(arrays)

    def kernel(pos_ref, x_ref, cos_ref, sin_ref, qk_ref, rot_ref, v_ref, prob_ref, gain_ref, head_gain_ref, ffn_ref, layer_ref, *refs):
        grad_refs, refs = refs[:nt], refs[nt:]
        piece_refs, refs = refs[:count], refs[count:]
        dqkv_ref = refs[0]
        part_refs, (w, out, db_ref, sems) = refs[1 : 1 + nt], refs[1 + nt :]
        f, t = pos_ref[0], pos_ref[1]

        def place(index, row, number):
            start = pl.multiple_of((f ^ index) * block + row, 16)
            return w.at[pl.ds(start, number), :]

        copies = start_fetch(pieces, piece_refs, place, sems)
        for d in range(nt):
            start = pl.multiple_of((t ^ d) * rows, 16)
            db_ref[pl.ds(start, rows), :] = grad_refs[d][:, :D]
        for copy in copies:
            copy.wait()
        cos, sin = cos_ref[...], sin_ref[...]
        head_gains = head_gain_ref[...]
        grad_att = dot(db_ref[...], w[:, 3 * width : 4 * width]).astype(BF16)
        gain_rows = [jnp.zeros((1, HD), F32), jnp.zeros((1, HD), F32)]
        for h in range(heads):
            span = slice(h * HD, (h + 1) * HD)
            query_low = rot_ref[:, span]
            key_low = rot_ref[:, width + h * HD : width + (h + 1) * HD]
            grad_out = grad_att[:, span]
            exact = prob_ref[h]
            grad_probs = dot_nt(grad_out, v_ref[:, span])
            row_terms = jnp.sum(exact * grad_probs, axis=-1, keepdims=True)
            grad_scores = (exact * (grad_probs - row_terms)).astype(BF16)
            dqkv_ref[:, 2 * width + h * HD : 2 * width + (h + 1) * HD] = dot_tn(
                exact.astype(BF16), grad_out
            ).astype(BF16)
            both = (dot(grad_scores, key_low), dot_tn(grad_scores, query_low))
            for which in range(2):
                span_w = slice(which * width + h * HD, which * width + (h + 1) * HD)
                grads = both[which] * (HD**-0.5)
                grads = grads * cos - half_turn(grads) * sin
                raw = qk_ref[:, span_w]
                inverse = rms_inverse(raw)
                gain_rows[which] = gain_rows[which] + jnp.sum(
                    grads * raw * inverse, axis=0, keepdims=True
                )
                dqkv_ref[:, span_w] = norm_backward(
                    raw, inverse, head_gains[2 + which : 3 + which], grads
                ).astype(BF16)
        grad_normed = dot_nt(dqkv_ref[...], w[:, : 3 * width])
        out[...] = grad_normed.astype(BF16)
        x = x_ref[...].astype(F32)
        row = jnp.sum(grad_normed * (x * rms_inverse(x)), axis=0, keepdims=True)
        lines = [row[:, k * SIDE : (k + 1) * SIDE] for row in (ffn_ref[0:1, :], row) for k in range(D // SIDE)]
        lines = lines + gain_rows
        gain_blocks = []
        for k in range(more // SIDE):
            own = lines[k * rows : (k + 1) * rows]
            blank = [jnp.zeros((rows - len(own), SIDE), F32)] if len(own) < rows else []
            gain_blocks.append(jnp.concatenate(own + blank, axis=0).astype(BF16))
        for d in range(nt):
            start = pl.multiple_of((t ^ d) * rows, 16)
            part_refs[d][:, :D] = out[pl.ds(start, rows), :]
            for k, gain_block in enumerate(gain_blocks):
                part_refs[d][:, D + k * SIDE : D + (k + 1) * SIDE] = gain_block
            part_refs[d][:, D + more :] = layer_ref[pl.ds(start, rows), :]

    results = pl.pallas_call(
        without(kernel, 12 + nt + count, len(deps)),
        out_shape=[
            shape((length, 3 * width), BF16),
        ]
        + [shape((rows, 2 * D + more), BF16)] * nt,
        in_specs=[SMEM] + [VMEM] * (11 + nt) + [HBM] * (count + len(deps)),
        out_specs=[VMEM] * (1 + nt),
        scratch_shapes=[
            pltpu.VMEM((D, columns), BF16),
            pltpu.VMEM((length, D), BF16),
            pltpu.VMEM((length, D), BF16),
            pltpu.SemaphoreType.DMA((len(pieces),)),
        ],
        compiler_params=params(60),
        cost_estimate=cost(0.1),
        name="attend_backward",
    )(
        pos, tokens, cosine, sine, qk, rot, values, probs, gains, head_gains, ffn_row, layer_sum,
        *grad_rows, *arrays, *deps,
    )
    return results[0], results[1:]


def projection_gradients(pos, normed, dqkv, nf, deps=()):
    length = normed.shape[0]
    block = D // nf
    width = dqkv.shape[1]

    def kernel(pos_ref, n1_ref, dqkv_ref, keep_ref, send_ref):
        for p in range(nf):
            start = pl.multiple_of((pos_ref[0] ^ p) * block, 128)
            to = (keep_ref if p % 2 == 0 else send_ref).at[p // 2]
            to[...] = dot_tn(n1_ref[:, pl.ds(start, block)], dqkv_ref[...]).astype(BF16)

    return pl.pallas_call(
        without(kernel, 3, len(deps)),
        out_shape=[shape((nf // 2, block, width), BF16)] * 2,
        in_specs=[SMEM, VMEM, VMEM] + [HBM] * len(deps),
        out_specs=[VMEM] * 2,
        compiler_params=params(40),
        cost_estimate=cost(0.1),
        name="projection_gradients",
    )(pos, normed, dqkv, *deps)


def output_gradients(pos, attended, grad_parts, normed_parts, gain_parts, group, nf, nt, deps=()):
    length, width = attended.shape
    rows = length // nt
    block = D // nf
    columns = width + SIDE
    more = gain_columns(rows)
    count = D // SIDE

    def kernel(pos_ref, att_ref, *refs):
        grad_refs, normed_refs, part_refs = refs[:nt], refs[nt : 2 * nt], refs[2 * nt : 3 * nt]
        keep_ref, send_ref, db, n2, held, gain_ref = refs[3 * nt :]
        f, t = pos_ref[0], pos_ref[1]
        for d in range(nt):
            start = pl.multiple_of((t ^ d) * rows, 16)
            db[pl.ds(start, rows), :] = grad_refs[d][...]
            n2[pl.ds(start, rows), :] = normed_refs[d][:, :D]
            held[t ^ d] = part_refs[d][:, D : D + more].astype(F32)
        total = held[0]
        for k in range(1, nt):
            total = total + held[k]
        for line in range(2 * count + 2):
            column, at = line // rows * SIDE, line % rows
            to = line // count if line < 2 * count else line - 2 * count + 2
            lane = line % count * SIDE if line < 2 * count else 0
            gain_ref[to : to + 1, lane : lane + SIDE] = total[at : at + 1, column : column + SIDE]
        lane = lanes((block, SIDE))
        sub = lax.broadcasted_iota(jnp.int32, (block, SIDE), 0)
        for p in range(nf):
            owner = f ^ p
            start = pl.multiple_of(owner * block, 128)
            to = (keep_ref if p % 2 == 0 else send_ref).at[p // 2]
            to[:, :width] = dot_tn(db[:, pl.ds(start, block)], att_ref[...]).astype(BF16)
            side = dot_tn(n2[:, pl.ds(start, block)], db[:, D:])
            for which in range(2):
                row = gain_ref[which : which + 1, pl.ds(start, block)]
                column = jnp.transpose(jnp.broadcast_to(row, (SIDE, block)))
                side = jnp.where(lane == EXPERTS + which, column, side)
            mine = (lane == owner * group + sub) & (sub < group)
            for which in range(2, 4):
                spread = jnp.where(mine, gain_ref[which : which + 1, :HD], 0.0)
                column = jnp.sum(spread, axis=1, keepdims=True)
                side = jnp.where(lane == EXPERTS + which, column, side)
            to[:, width:] = side.astype(BF16)

    return pl.pallas_call(
        without(kernel, 2 + 3 * nt, len(deps)),
        out_shape=[shape((nf // 2, block, columns), BF16)] * 2,
        in_specs=[SMEM] + [VMEM] * (1 + 3 * nt) + [HBM] * len(deps),
        out_specs=[VMEM] * 2,
        scratch_shapes=[
            pltpu.VMEM((length, D + SIDE), BF16),
            pltpu.VMEM((length, D), BF16),
            pltpu.VMEM((nt, rows, more), F32),
            pltpu.VMEM((8, D), F32),
        ],
        compiler_params=params(40),
        cost_estimate=cost(0.1),
        name="output_gradients",
    )(pos, attended, *grad_parts, *normed_parts, *gain_parts, *deps)


def gain_columns(rows):
    return SIDE * -(-(2 * D // SIDE + 2) // rows)


def norm_and_route(pos, tokens, routes, parts, gains, side, nt, deps=()):
    rows = tokens.shape[0] // nt
    top = routes.shape[1]

    def kernel(pos_ref, x_ref, route_ref, gain_ref, side_ref, *refs):
        part_refs, (h_ref, next_ref, gate_ref) = refs[:nt], refs[nt:]
        h = x_ref[...].astype(F32)
        for ref in part_refs:
            h = h + ref[...].astype(F32)
        h_ref[...] = h
        n2 = (h * rms_inverse(h) * gain_ref[1:2]).astype(BF16)
        next_ref[:, :D] = n2
        logits = dot(n2, side_ref[...])
        lane = lanes((rows, SIDE))
        chosen = route_ref[:, 0:1] == lane
        for j in range(1, top):
            chosen = chosen | (route_ref[:, j : j + 1] == lane)
        highest = jnp.max(jnp.where(chosen, logits, -jnp.inf), axis=-1, keepdims=True)
        shifted = jnp.where(chosen, jnp.exp(jnp.where(chosen, logits - highest, 0.0)), 0.0)
        gates = shifted / jnp.sum(shifted, axis=-1, keepdims=True)
        gate_ref[...] = gates
        first = gates.astype(BF16).astype(F32)
        rest = (gates - first).astype(BF16).astype(F32)
        next_ref[:, D:] = (first + pltpu.roll(rest, EXPERTS, 1)).astype(BF16)

    whole = lambda i, pos: (0, 0)
    mine = lambda i, pos: (pos[1], 0)
    return pl.pallas_call(
        without(kernel, 5 + nt, len(deps)),
        out_shape=[shape((rows, D), F32), shape((rows, D + SIDE), BF16), shape((rows, SIDE), F32)],
        grid_spec=pltpu.PrefetchScalarGridSpec(
            num_scalar_prefetch=1,
            grid=(1,),
            in_specs=[
                pl.BlockSpec((rows, D), mine),
                pl.BlockSpec((rows, top), mine),
                pl.BlockSpec((8, D), whole),
                pl.BlockSpec((D, SIDE), whole),
            ]
            + [pl.BlockSpec((rows, D), whole)] * nt
            + [HBM] * len(deps),
            out_specs=[
                pl.BlockSpec((rows, D), whole),
                pl.BlockSpec((rows, D + SIDE), whole),
                pl.BlockSpec((rows, SIDE), whole),
            ],
        ),
        compiler_params=params(),
        cost_estimate=cost(100),
        name="norm_and_route",
    )(pos, tokens, routes, gains, side, *parts, *deps)


def norm_back(pos, cotangent, parts, h, gates, gains, side, nt, deps=()):
    rows = h.shape[0]

    def kernel(pos_ref, cot_ref, h_ref, gate_ref, gain_ref, side_ref, *refs):
        part_refs, (dh_ref, db_ref, row_ref) = refs[:nt], refs[nt:]
        total = part_refs[0][...].astype(F32)
        for ref in part_refs[1:]:
            total = total + ref[...].astype(F32)
        pair = total[:, D:]
        pair = pair + pltpu.roll(pair, EXPERTS, 1)
        gates = gate_ref[...]
        grads = gates * (pair - jnp.sum(gates * pair, axis=-1, keepdims=True))
        low = grads.astype(BF16)
        dn2 = total[:, :D] + dot_nt(low, side_ref[...])
        h = h_ref[...]
        inverse = rms_inverse(h)
        gain_row = jnp.sum(dn2 * h * inverse, axis=0, keepdims=True)
        row_ref[...] = jnp.broadcast_to(gain_row, (8, D))
        dh = cot_ref[...].astype(F32) + norm_backward(h, inverse, gain_ref[1:2], dn2)
        dh_ref[...] = dh
        db_ref[:, :D] = dh.astype(BF16)
        db_ref[:, D:] = low

    whole = lambda i, pos: (0, 0)
    mine = lambda i, pos: (pos[1], 0)
    return pl.pallas_call(
        without(kernel, 6 + nt, len(deps)),
        out_shape=[shape((rows, D), F32), shape((rows, D + SIDE), BF16), shape((8, D), F32)],
        grid_spec=pltpu.PrefetchScalarGridSpec(
            num_scalar_prefetch=1,
            grid=(1,),
            in_specs=[
                pl.BlockSpec((rows, D), mine),
                pl.BlockSpec((rows, D), whole),
                pl.BlockSpec((rows, SIDE), whole),
                pl.BlockSpec((8, D), whole),
                pl.BlockSpec((D, SIDE), whole),
            ]
            + [pl.BlockSpec((rows, D + SIDE), whole)] * nt
            + [HBM] * len(deps),
            out_specs=[
                pl.BlockSpec((rows, D), whole),
                pl.BlockSpec((rows, D + SIDE), whole),
                pl.BlockSpec((8, D), whole),
            ],
        ),
        compiler_params=params(),
        cost_estimate=cost(100),
        name="norm_back",
    )(pos, cotangent, h, gates, gains, side, *parts, *in_hbm(deps))


def last_rows(pos, tokens, parts, dh, h, gains, nt, deps=()):
    rows = dh.shape[0]
    columns = parts[0].shape[1]

    def kernel(pos_ref, x_ref, dh_ref, h_ref, gain_ref, *refs):
        part_refs, out_ref = refs[:nt], refs[nt]
        total = part_refs[0][:, :D].astype(F32)
        layer = h_ref[...] + part_refs[0][:, columns - D :].astype(F32)
        for ref in part_refs[1:]:
            total = total + ref[:, :D].astype(F32)
            layer = layer + ref[:, columns - D :].astype(F32)
        x = x_ref[...].astype(F32)
        out_ref[:, :D] = (
            dh_ref[...] + norm_backward(x, rms_inverse(x), gain_ref[0:1], total)
        ).astype(BF16)
        out_ref[:, D:] = layer.astype(BF16)

    whole = lambda i, pos: (0, 0)
    return pl.pallas_call(
        without(kernel, 5 + nt, len(deps)),
        out_shape=shape((rows, 2 * D), BF16),
        grid_spec=pltpu.PrefetchScalarGridSpec(
            num_scalar_prefetch=1,
            grid=(1,),
            in_specs=[
                pl.BlockSpec((rows, D), lambda i, pos: (pos[1], 0)),
                pl.BlockSpec((rows, D), whole),
                pl.BlockSpec((rows, D), whole),
                pl.BlockSpec((8, D), whole),
            ]
            + [pl.BlockSpec((rows, columns), whole)] * nt
            + [HBM] * len(deps),
            out_specs=pl.BlockSpec((rows, 2 * D), whole),
        ),
        compiler_params=params(60),
        cost_estimate=cost(100),
        name="last_rows",
    )(pos, tokens, dh, h, gains, *parts, *deps)


def place_rows(pos, parts):
    nt = len(parts)
    rows, columns = parts[0].shape
    half = columns // 2

    def kernel(pos_ref, *refs):
        left_ref, right_ref = refs[nt:]
        for d in range(nt):
            start = pl.multiple_of((pos_ref[1] ^ d) * rows, 16)
            left_ref[pl.ds(start, rows), :] = refs[d][:, :half]
            right_ref[pl.ds(start, rows), :] = refs[d][:, half:]

    return pl.pallas_call(
        kernel,
        out_shape=[shape((rows * nt, half), parts[0].dtype)] * 2,
        in_specs=[SMEM] + [VMEM] * nt,
        out_specs=[VMEM] * 2,
        compiler_params=params(),
        cost_estimate=cost(0.1),
        name="place_rows",
    )(pos, *parts)


def spread_rows(slots, source, target, pair, number, cut):
    for begin in range(0, source.shape[2], cut):
        span = slice(begin, min(begin + cut, source.shape[2]))
        two = [dot_tn(slots[2 * pair + k], source[2 * pair + k, :, span]) for k in range(2)]
        for e in range(number):
            joined = jnp.concatenate([rows[e * CAP : (e + 1) * CAP] for rows in two], axis=0)
            target(e, span, joined)


def sum_rows(slots, results, target, pair, number, total, cut):
    at = slice(pair * 2 * CAP, (pair + 1) * 2 * CAP)
    for begin in range(0, total, cut):
        span = slice(begin, min(begin + cut, total))
        blocks = [results[e, at, span].astype(F32) for e in range(number)]
        for k in range(2):
            rows = jnp.concatenate([b[k * CAP : (k + 1) * CAP] for b in blocks], axis=0)
            target[2 * pair + k, :, span] = dot(slots[2 * pair + k], rows.astype(BF16)).astype(BF16)


def route_cotangent(pos, pieces, weights, nf, top, deps=()):
    number = weights.shape[0]
    length = sum(rows for index, _, _, _, rows in pieces if index == 0)
    slots = number * CAP
    arrays = arrays_of(pieces)
    count = len(arrays)

    def kernel(pos_ref, *refs):
        piece_refs, (slot_ref, rows_ref, cot, spread, sems, out_sems) = refs[:count], refs[count:]
        f = pos_ref[0]
        copies = start_fetch(
            pieces, piece_refs, lambda i, row, n: cot.at[i, pl.ds(row, n), :], sems, f
        )
        column = lanes((length, slots))
        expert = jnp.zeros((length, slots), jnp.int32)
        for k in range(1, number):
            expert = expert + (column >= k * CAP).astype(jnp.int32)
        rank = (column - expert * CAP + 1).astype(F32)
        expert = (expert + f * number).astype(F32)
        lower = (
            lax.broadcasted_iota(jnp.int32, (length, length), 0) >= lanes((length, length))
        ).astype(F32).astype(BF16)
        for copy in copies:
            copy.wait()

        def leave(pair):
            span = pl.ds(pl.multiple_of(pair * 2 * CAP, 16), 2 * CAP)
            return pltpu.make_async_copy(
                spread.at[:, span, :], rows_ref.at[:, span, :], out_sems.at[pair]
            )

        @pl.loop(0, nf // 2)
        def _(pair):
            for s in (2 * pair, 2 * pair + 1):
                named = cot[s, :, D:].astype(F32)
                hit = named[:, 0:1] == expert
                for j in range(1, top):
                    hit = hit | (named[:, j : j + 1] == expert)
                hit = jnp.where(hit, 1.0, 0.0)
                so_far = dot(lower, hit.astype(BF16))
                slot_ref[s] = jnp.where((so_far == rank) & (hit > 0.0), 1.0, 0.0).astype(BF16)
            at = pl.ds(pl.multiple_of(pair * 2 * CAP, 16), 2 * CAP)

            def put(k, span, rows):
                spread[k, at, span] = rows.astype(BF16)

            spread_rows(slot_ref, cot.at[:, :, :D], put, pair, number, 512)
            leave(pair).start()

        for pair in range(nf // 2):
            leave(pair).wait()

    return pl.pallas_call(
        without(kernel, 1 + count, len(deps)),
        out_shape=[
            shape((nf, length, slots), BF16),
            shape((number, nf * CAP, D), BF16),
        ],
        in_specs=[SMEM] + [HBM] * (count + len(deps)),
        out_specs=[VMEM, HBM],
        scratch_shapes=[
            pltpu.VMEM((nf, length, D + SIDE), BF16),
            pltpu.VMEM((number, nf * CAP, D), BF16),
            pltpu.SemaphoreType.DMA((len(pieces),)),
            pltpu.SemaphoreType.DMA((nf // 2,)),
        ],
        compiler_params=params(60),
        cost_estimate=cost(0.1),
        name="route_cotangent",
    )(pos, *arrays, *deps)


def down_back(grad_rows, weights, deps=()):
    number, filled, _ = grad_rows.shape
    width = weights.shape[3]

    def kernel(rows_ref, w_ref, out_ref):
        for k in range(2):
            out_ref[k] = dot(rows_ref[k], w_ref[k, 0])

    return pl.pallas_call(
        without(kernel, 2, len(deps)),
        out_shape=shape((number, filled, width), F32),
        grid=(number // 2,),
        in_specs=[
            pl.BlockSpec((2, filled, D), lambda e: (e, 0, 0)),
            pl.BlockSpec((2, 1, D, width), lambda e: (e, 2, 0, 0)),
        ]
        + [HBM] * len(deps),
        out_specs=pl.BlockSpec((2, filled, width), lambda e: (e, 0, 0)),
        compiler_params=params(60),
        cost_estimate=cost(0.1),
        name="down_back",
    )(grad_rows, weights, *deps)


def run_experts(pos, pieces, slot_table, down, weights, nf, cut):
    number, _, _, width = weights.shape
    length, slots = slot_table.shape[1:]
    filled = nf * CAP
    arrays = arrays_of(pieces)
    count = len(arrays)

    def kernel(pos_ref, slot_ref, down_ref, gate_w, up_w, *refs):
        piece_refs, refs = refs[:count], refs[count:]
        rows_ref, dg_ref, du_ref, hidden_ref = refs[:4]
        sums_refs = (refs[4:6], refs[6:8])
        wide, spread, gates, results, sems, rows_sem, out_sems = refs[8:]
        e = pl.program_id(0)
        f = pos_ref[0]
        rows_out = pltpu.make_async_copy(spread, rows_ref, rows_sem)

        @pl.when(e == 0)
        def _():
            copies = start_fetch(
                pieces, piece_refs, lambda i, row, n: wide.at[i, pl.ds(row, n), :], sems
            )
            for pair in range(nf // 2):
                for (index, _, _, _, _), copy in zip(pieces, copies):
                    if index // 2 == pair:
                        copy.wait()
                at = slice(pair * 2 * CAP, (pair + 1) * 2 * CAP)

                def put(k, span, rows):
                    if span.start < D:
                        spread[k, at, span] = rows.astype(BF16)
                    else:
                        lane = lanes((2 * CAP, SIDE))
                        own = f * number + k
                        gate = jnp.where((lane == own) | (lane == own + EXPERTS), rows, 0.0)
                        gates[k, at, :] = jnp.broadcast_to(
                            jnp.sum(gate, axis=-1, keepdims=True), (2 * CAP, SIDE)
                        )

                spread_rows(slot_ref, wide, put, pair, number, 512)
            rows_out.start()

        for k in range(2):
            index = 2 * e + k
            rows = spread[index]
            first, second = gate_w[k, 0], up_w[k, 0]
            gate_pre = dot(rows, first)
            up_pre = dot(rows, second)
            gate = gates[index][:, 0:1]
            sigma = jax.nn.sigmoid(gate_pre)
            swish = gate_pre * sigma
            hidden = (swish * up_pre).astype(BF16).astype(F32)
            hidden_ref[k] = (gate * hidden).astype(BF16)
            unscaled = down_ref[k]
            grad_hidden = gate * unscaled
            dg = (grad_hidden * up_pre * sigma * (1.0 + gate_pre * (1.0 - sigma))).astype(BF16)
            du = (grad_hidden * swish).astype(BF16)
            dg_ref[k] = dg
            du_ref[k] = du
            results[index, :, :D] = (dot_nt(dg, first) + dot_nt(du, second)).astype(BF16)
            pair_grad = jnp.sum(unscaled * hidden, axis=-1, keepdims=True)
            high = pair_grad.astype(BF16).astype(F32)
            lane = lanes((filled, SIDE))
            own = f * number + index
            results[index, :, D:] = jnp.where(
                lane == own, high, jnp.where(lane == own + EXPERTS, pair_grad - high, 0.0)
            ).astype(BF16)

        @pl.when(e == number // 2 - 1)
        def _():
            copies = []
            for pair in range(nf // 2):
                sum_rows(slot_ref, results, wide, pair, number, D + SIDE, 512)
                for k, to in enumerate(sums_refs):
                    index = 2 * pair + k
                    for g, span in enumerate((pl.ds(0, cut), pl.ds(cut, length - cut))):
                        copy = pltpu.make_async_copy(
                            wide.at[index, span, :], to[g].at[pair], out_sems.at[2 * index + g]
                        )
                        copy.start()
                        copies.append(copy)
            for copy in copies:
                copy.wait()
            rows_out.wait()

    return pl.pallas_call(
        kernel,
        out_shape=[
            shape((number, filled, D), BF16),
            shape((number, filled, width), BF16),
            shape((number, filled, width), BF16),
            shape((number, filled, width), BF16),
        ]
        + [shape((nf // 2, number, D + SIDE), BF16) for number in (cut, length - cut)] * 2,
        grid_spec=pltpu.PrefetchScalarGridSpec(
            num_scalar_prefetch=1,
            grid=(number // 2,),
            in_specs=[
                pl.BlockSpec((nf, length, slots), lambda e, pos: (0, 0, 0)),
                pl.BlockSpec((2, filled, width), lambda e, pos: (e, 0, 0)),
                pl.BlockSpec((2, 1, D, width), lambda e, pos: (e, 0, 0, 0)),
                pl.BlockSpec((2, 1, D, width), lambda e, pos: (e, 1, 0, 0)),
            ]
            + [HBM] * count,
            out_specs=[
                HBM,
                pl.BlockSpec((2, filled, width), lambda e, pos: (e, 0, 0)),
                pl.BlockSpec((2, filled, width), lambda e, pos: (e, 0, 0)),
                pl.BlockSpec((2, filled, width), lambda e, pos: (e, 0, 0)),
            ]
            + [HBM] * 4,
            scratch_shapes=[
                pltpu.VMEM((nf, length, D + SIDE), BF16),
                pltpu.VMEM((number, filled, D), BF16),
                pltpu.VMEM((number, filled, SIDE), F32),
                pltpu.VMEM((number, filled, D + SIDE), BF16),
                pltpu.SemaphoreType.DMA((len(pieces),)),
                pltpu.SemaphoreType.DMA,
                pltpu.SemaphoreType.DMA((2 * nf,)),
            ],
        ),
        compiler_params=params(60),
        cost_estimate=cost(5),
        name="run_experts",
    )(pos, slot_table, down, weights, weights, *arrays)


def expert_outputs(pos, slot_table, hidden, weights, nt, deps=()):
    number, filled, width = hidden.shape
    nf, length, slots = slot_table.shape

    rows = length // nt

    def kernel(pos_ref, slot_ref, hidden_ref, w_ref, out_ref, results, out, sems):
        e = pl.program_id(0)
        for k in range(2):
            results[2 * e + k] = dot_nt(hidden_ref[k], w_ref[k, 0]).astype(BF16)

        @pl.when(e == number // 2 - 1)
        def _():
            copies = []
            for pair in range(nf // 2):
                sum_rows(slot_ref, results, out, pair, number, D, 512)
                for index in (2 * pair, 2 * pair + 1):
                    for d in range(nt):
                        start = pl.multiple_of((pos_ref[1] ^ d) * rows, 16)
                        copy = pltpu.make_async_copy(
                            out.at[index, pl.ds(d * rows, rows), :],
                            out_ref.at[pos_ref[0] ^ index, pl.ds(start, rows), :],
                            sems.at[index * nt + d],
                        )
                        copy.start()
                        copies.append(copy)
            for copy in copies:
                copy.wait()

    return pl.pallas_call(
        without(kernel, 4, len(deps)),
        out_shape=shape((nf, length, D), BF16),
        grid_spec=pltpu.PrefetchScalarGridSpec(
            num_scalar_prefetch=1,
            grid=(number // 2,),
            in_specs=[
                pl.BlockSpec((nf, length, slots), lambda e, pos: (0, 0, 0)),
                pl.BlockSpec((2, filled, width), lambda e, pos: (e, 0, 0)),
                pl.BlockSpec((2, 1, D, width), lambda e, pos: (e, 2, 0, 0)),
            ]
            + [HBM] * len(deps),
            out_specs=HBM,
            scratch_shapes=[
                pltpu.VMEM((number, filled, D), BF16),
                pltpu.VMEM((nf, length, D), BF16),
                pltpu.SemaphoreType.DMA((nf * nt,)),
            ],
        ),
        compiler_params=params(48),
        cost_estimate=cost(0.1),
        name="expert_outputs",
    )(pos, slot_table, hidden, weights, *deps)


def expert_gradients(rows, grad_rows, dg, du, hidden, first, number, so_far=None, deps=()):
    everyone, filled, width = dg.shape

    def kernel(rows_ref, grad_ref, dg_ref, du_ref, hidden_ref, *refs):
        out_ref, done_ref = refs
        done_ref[...] = jnp.zeros_like(done_ref)
        rows = rows_ref[0]
        out_ref[0, 0] = dot_tn(rows, dg_ref[0])
        out_ref[0, 1] = dot_tn(rows, du_ref[0])
        out_ref[0, 2] = dot_tn(grad_ref[0], hidden_ref[0])

    tall = pl.BlockSpec((1, filled, D), lambda e: (first + e, 0, 0))
    thin = pl.BlockSpec((1, filled, width), lambda e: (first + e, 0, 0))
    before = [] if so_far is None else [so_far]
    return pl.pallas_call(
        without(kernel, 5, len(before) + len(deps)),
        out_shape=[shape((everyone, 3, D, width), F32), shape((8, SIDE), F32)],
        grid=(number,),
        in_specs=[tall, tall, thin, thin, thin] + [HBM] * (len(before) + len(deps)),
        out_specs=[
            pl.BlockSpec((1, 3, D, width), lambda e: (first + e, 0, 0, 0)),
            pl.BlockSpec((8, SIDE), lambda e: (0, 0)),
        ],
        input_output_aliases={5: 0} if before else {},
        compiler_params=params(48),
        cost_estimate=cost(0.1),
        name="expert_gradients",
    )(rows, grad_rows, dg, du, hidden, *before, *deps)


def on_device(
    nf,
    nt,
    tokens,
    cotangent,
    routes,
    w_query,
    w_key,
    w_value,
    w_output,
    w_router,
    attn_gain,
    ffn_gain,
    query_gain,
    key_gain,
    expert_weights,
):
    length = tokens.shape[0]
    rows = length // nt
    block = D // nf
    group = query_gain.shape[0]
    top = routes.shape[1]
    f = lax.axis_index("fsdp").astype(jnp.int32)
    t = lax.axis_index("tensor").astype(jnp.int32)
    pos = jnp.stack([f, t])

    def placed(gain):
        return lax.dynamic_update_slice(jnp.zeros((block,), BF16), gain, (f * group,))[:, None]

    columns = [
        w_query,
        w_key,
        w_value,
        w_output,
        w_router,
        attn_gain[:, None],
        ffn_gain[:, None],
        placed(query_gain),
        placed(key_gain),
        jnp.zeros((block, SIDE - EXPERTS - 4), BF16),
    ]
    number = expert_weights.shape[0]
    cut = 2 * rows

    def around(block):
        return [block] + [swap(block, "tensor", nt, d) for d in range(1, nt)]

    def sent(parts):
        return [parts[0]] + [swap(parts[d], "tensor", nt, d) for d in range(1, nt)]

    if nf == 8:
        packed = [
            jnp.concatenate([part[half : half + block // 2] for part in columns], axis=1)
            for half in (0, block // 2)
        ]
        weights_near = [gather_near(part, nf) for part in packed]
    else:
        packed = jnp.concatenate(columns, axis=1)

    wide_cot = jnp.concatenate(
        [cotangent, routes.astype(BF16), jnp.zeros((length, SIDE - top), BF16)], axis=1
    )
    wide_cot = jnp.concatenate(
        [lax.dynamic_slice_in_dim(wide_cot, (t ^ d) * rows, rows, 0) for d in range(nt)], axis=0
    )
    position = jnp.arange(length, dtype=F32)[:, None]
    inverse = ROPE_BASE ** (-jnp.arange(HD // 2, dtype=F32) / (HD // 2))
    angles = position * inverse[None, :]
    cosine = jnp.concatenate([jnp.cos(angles)] * 2, axis=1)
    sine = jnp.concatenate([-jnp.sin(angles), jnp.sin(angles)], axis=1)

    if nf == 8:
        weights = gather_two(packed, weights_near, nf)
        wide_cot = join(
            [wide_cot],
            weights_near[0]
            + weights_near[1]
            + [w[2] for w in weights if w[0] == nf - 2]
            + [cosine, sine],
        )
    else:
        weights = gather_rest(packed, gather_near(packed, nf), nf)
    all_cot = lax.all_gather(wide_cot, "fsdp", axis=0, tiled=True)
    cot = [(p, 0, all_cot, None, length) for p in range(nf)]
    saved, parts = attend_forward(pos, tokens, cosine, sine, weights, nf, nt)
    normed_one, _, _, _, _, attended, side, gains, _ = saved
    parts = sent(parts)
    h, normed_two, gates = norm_and_route(pos, tokens, routes, parts, gains, side, nt)

    normed_parts = around(normed_two)
    if nf == 8:
        blocks = [join(normed_parts[:2])]
        near = [gather_near(blocks[0], nf)]
        slot_table, cot_rows = route_cotangent(pos, cot, expert_weights, nf, top, deps=blocks)
        blocks.append(join(normed_parts[2:], deps=[slot_table]))
        near.append(gather_near(blocks[1], nf))
        down = down_back(cot_rows, expert_weights, deps=blocks[1:])
        sources = [near[0][1]] + list(relay(near[1][:1], [down]))
        n2_pieces = gather_two(blocks, near, nf, sources)
    else:
        slot_table, cot_rows = route_cotangent(pos, cot, expert_weights, nf, top)
        down = down_back(cot_rows, expert_weights)
        joined = join(normed_parts)
        n2_pieces = gather_rest(joined, gather_near(joined, nf), nf)
    n2_rows, dg, du, hidden, keep_near, keep_far, send_near, send_far = run_experts(
        pos, n2_pieces, slot_table, down, expert_weights, nf, cut
    )

    far, near = Reduce(keep_far, send_far, nf), Reduce(keep_near, send_near, nf)
    began = far.first() + near.first()
    outputs = expert_outputs(pos, slot_table, hidden, expert_weights, nt, deps=began)
    layer_sum = lax.psum_scatter(
        outputs.reshape(nf * length, D), "fsdp", scatter_dimension=0, tiled=True
    )
    went = far.second(deps=[outputs], micros=20)
    near.second(deps=went, micros=20)
    far_rows = list(far.rows(nt - 2))
    near_rows = list(near.rows(2, deps=far_rows[:1]))
    grad_parts = sent(near_rows + far_rows)
    each = number // 2

    def expert_part(k, deps=()):
        return expert_gradients(
            n2_rows, cot_rows, dg, du, hidden, k * each, each, grad_experts, deps
        )

    grad_experts = None
    grad_experts, done = expert_part(0, near_rows[:1])
    dh, db, ffn_row = norm_back(
        pos, cotangent, grad_parts, h, gates, gains, side, nt, deps=[done]
    )
    db_parts = around(db)
    grad_experts, done = expert_part(1, [db])
    dqkv, parts = attend_backward(
        pos, db_parts, ffn_row, layer_sum, weights, saved, tokens, cosine, sine, nf, nt,
        deps=[done],
    )
    parts = sent(parts)
    keep, send = projection_gradients(pos, normed_one, dqkv, nf)
    projections = Reduce(keep, send, nf)
    both_rows = last_rows(pos, tokens, parts, dh, h, gains, nt, deps=[keep])
    gathered = lax.all_gather(both_rows, "tensor", axis=0, tiled=True)
    pairs = projections.first(deps=[both_rows])
    keep, send = output_gradients(
        pos, attended, db_parts, normed_parts, parts, group, nf, nt, deps=pairs
    )
    output = Reduce(keep, send, nf)
    output.first()
    projections.second()
    output.second()
    width = attended.shape[1]
    grad_query, grad_key, grad_value = projections.columns([width] * 3)
    grad_output, side_grads = output.columns([width], SIDE)
    grad_tokens, layer_out = halve(gathered, deps=[grad_output, grad_query])
    return (
        layer_out,
        grad_tokens,
        grad_query,
        grad_key,
        grad_value,
        grad_output,
        side_grads[:EXPERTS].T,
        side_grads[EXPERTS + 1],
        side_grads[EXPERTS],
        side_grads[EXPERTS + 2, :group],
        side_grads[EXPERTS + 3, :group],
        grad_experts,
    )


def solution(mesh):
    nf, nt = mesh.shape["fsdp"], mesh.shape["tensor"]
    rows, both, line = P("fsdp", None), P("fsdp", "tensor"), P("fsdp")
    experts = P("fsdp", None, None, "tensor")
    return jax.shard_map(
        functools.partial(on_device, nf, nt),
        mesh=mesh,
        in_specs=(rows, rows, rows, both, both, both, both, rows, line, line, line, line, experts),
        out_specs=(rows, rows, both, both, both, both, rows, line, line, line, line, experts),
        check_vma=False,
    )
```

profile of v0, /device:TPU:0, one launch (start us, length us, event | category | flops | bytes accessed | tf_op | source)
XLA Modules:
  0.0 434.5 jit_solution(10470417097994121652)
XLA Ops:
  21.3 9.5 %collective-permute-done.3.refs_8_.refs_2_.refs_20_ = bf16[128,2176]{1,0:T(8,128)(2,1)} collective-permute-done((bf16[128,2176]{1,0:T(8,128)(2,1)S(1)}, bf16[128,2176]{1,0:T(8,128)(2,1)}, u32[]{:S(2)}, u32[]{:S(2)}) %collective-permute-start.3) | collective-permute-done | bytes 557088 | tf_op jit(solution)/shard_map/ppermute | solution.py:80
  36.8 8.8 %collective-permute-done.1.refs_6_.refs_1_.refs_18_ = bf16[128,2176]{1,0:T(8,128)(2,1)} collective-permute-done((bf16[128,2176]{1,0:T(8,128)(2,1)S(1)}, bf16[128,2176]{1,0:T(8,128)(2,1)}, u32[]{:S(2)}, u32[]{:S(2)}) %collective-permute-start.1) | collective-permute-done | bytes 557088 | tf_op jit(solution)/shard_map/ppermute | solution.py:80
  45.6 10.4 %collective-permute-done.5.refs_10_.refs_5_.refs_22_ = bf16[128,2176]{1,0:T(8,128)(2,1)S(1)} collective-permute-done((bf16[128,2176]{1,0:T(8,128)(2,1)}, bf16[128,2176]{1,0:T(8,128)(2,1)S(1)}, u32[]{:S(2)}, u32[]{:S(2)}) %collective-permute-start.5) | collective-permute-done | bytes 557088 | tf_op jit(solution)/shard_map/ppermute | solution.py:80
  67.8 10.1 %attend_forward.1 = (bf16[256,2048]{1,0:T(8,128)(2,1)}, f32[256,1024]{1,0:T(8,128)}, bf16[256,1024]{1,0:T(8,128)(2,1)}, bf16[256,512]{1,0:T(8,128)(2,1)}, f32[4,...) custom-call(s32[2]{0:T(128)} %pad_add_fusion.refs_0_.pos_ref, ...), custom_call_target="tpu_custom_call" | custom-call | flops 5000000000 | bytes 15000000 | tf_op jit(solution)/shard_map/attend_forward/pallas_call | solution.py:507
  82.5 9.1 %collective-permute-done.14.refs_6_ = bf16[64,2048]{1,0:T(8,128)(2,1)S(1)} collective-permute-done((bf16[64,2048]{1,0:T(8,128)(2,1)}, bf16[64,2048]{1,0:T(8,128)(2,1)S(1)}, u32[]{:S(2)}, u32[]{:S(2)}) %collective-permute-start.14) | collective-permute-done | bytes 262176 | tf_op jit(solution)/shard_map/ppermute | solution.py:80
  91.6 9.6 %collective-permute-done.15.refs_7_ = bf16[64,2048]{1,0:T(8,128)(2,1)S(1)} collective-permute-done((bf16[64,2048]{1,0:T(8,128)(2,1)}, bf16[64,2048]{1,0:T(8,128)(2,1)S(1)}, u32[]{:S(2)}, u32[]{:S(2)}) %collective-permute-start.15) | collective-permute-done | bytes 262176 | tf_op jit(solution)/shard_map/ppermute | solution.py:80
  106.8 5.1 %collective-permute-start.17 = (bf16[64,2176]{1,0:T(8,128)(2,1)S(1)}, bf16[64,2176]{1,0:T(8,128)(2,1)S(1)}, u32[]{:S(2)}, u32[]{:S(2)}) collective-permute-start(bf16[64,2176]{1,0:T(8,128)(2,1)S(1)} %get-tuple-element.89.refs_0_.refs_6_), channel_id=1, source_target_pairs={{0,1},{1,0},{2,3},{3,2},{4,5},{5,4},{6,7},{7,6},{8,9},{9,8},{10,11... | collective-permute-start | bytes 835592 | tf_op jit(solution)/shard_map/ppermute | solution.py:80
  114.3 4.7 %collective-permute-done.17.refs_1_.refs_7_ = bf16[64,2176]{1,0:T(8,128)(2,1)S(1)} collective-permute-done((bf16[64,2176]{1,0:T(8,128)(2,1)S(1)}, bf16[64,2176]{1,0:T(8,128)(2,1)S(1)}, u32[]{:S(2)}, u32[]{:S(2)}) %collective-permute-start.17) | collective-permute-done | bytes 278560 | tf_op jit(solution)/shard_map/ppermute | solution.py:80
  124.0 14.7 %route_cotangent.1 = (bf16[8,256,320]{2,1,0:T(8,128)(2,1)}, bf16[8,320,2048]{2,1,0:T(8,128)(2,1)}) custom-call(s32[2]{0:T(128)} %pad_add_fusion.refs_0_.pos_ref, bf16[2048,2176]{1,0:T(8,128)(2,1)} %all-gather.3.cloned.1.call-done.refs_1_, bf16[128,2176]{1,0:T(8,128)(2,1)} %joins.5.refs_2_.refs_0_), custom_call_target="tpu_custom_call" | custom-call | flops 100000000 | bytes 300000 | tf_op jit(solution)/shard_map/route_cotangent/pallas_call | solution.py:961
  144.1 9.3 %down_back.1.refs_1_.down_ref = f32[8,320,256]{2,1,0:T(8,128)} custom-call(bf16[8,320,2048]{2,1,0:T(8,128)(2,1)} %get-tuple-element.91.refs_0_.refs_1_, bf16[8,3,2048,256]{3,2,1,0:T(8,128)(2,1)} %refs_3_.1, bf16[128,2176]{1,0:T(8,128)(2,1)} %joins.6.refs_2_.refs_8_), custom_call_target="tpu_custom_call" | custom-call | flops 100000000 | bytes 300000 | tf_op jit(solution)/shard_map/down_back/pallas_call | solution.py:989
  153.4 3.8 collective-permute-done.28.refs_0_.refs_10_
  161.2 3.7 collective-permute-done.25.refs_6_
  165.5 7.4 %collective-permute-done.30.refs_12_ = bf16[128,2176]{1,0:T(8,128)(2,1)} collective-permute-done((bf16[128,2176]{1,0:T(8,128)(2,1)S(1)}, bf16[128,2176]{1,0:T(8,128)(2,1)}, u32[]{:S(2)}, u32[]{:S(2)}) %collective-permute-start.30) | collective-permute-done | bytes 557088 | tf_op jit(solution)/shard_map/ppermute | solution.py:80
  172.9 7.3 %collective-permute-done.32.refs_14_ = bf16[128,2176]{1,0:T(8,128)(2,1)S(1)} collective-permute-done((bf16[128,2176]{1,0:T(8,128)(2,1)}, bf16[128,2176]{1,0:T(8,128)(2,1)S(1)}, u32[]{:S(2)}, u32[]{:S(2)}) %collective-permute-start.32) | collective-permute-done | bytes 557088 | tf_op jit(solution)/shard_map/ppermute | solution.py:80
  182.3 31.6 %run_experts.1 = (bf16[8,320,2048]{2,1,0:T(8,128)(2,1)}, bf16[8,320,256]{2,1,0:T(8,128)(2,1)}, bf16[8,320,256]{2,1,0:T(8,128)(2,1)}, bf16[8,320,256]{2,1,0:T(8,1...) custom-call(s32[2]{0:T(128)} %pad_add_fusion.refs_0_.pos_ref, ...), custom_call_target="tpu_custom_call" | custom-call | flops 5000000000 | bytes 15000000 | tf_op jit(solution)/shard_map/run_experts/pallas_call | solution.py:1089
  214.5 4.0 collective-permute-done.37.refs_1_
  228.3 12.9 %expert_outputs.1.refs_4_ = bf16[8,256,2048]{2,1,0:T(8,128)(2,1)} custom-call(s32[2]{0:T(128)S(1)} %copy-done.37, bf16[8,256,320]{2,1,0:T(8,128)(2,1)S(1)} %copy-done.4, bf16[8,320,256]{2,1,0:T(8,128)(2,1)S(1)} %copy-done.5, bf16[8,3,2048,256]{3,2,1,0:T(8,128)(2,1)} %refs_3_.1, bf16[2,64,2176]{2,1,0:T(8,128)(2,1)} %get-tuple-element.98.refs_4_, ...), custom_call_target="tpu_custom_call" | custom-call | flops 100000000 | bytes 300000 | tf_op jit(solution)/shard_map/expert_outputs/pallas_call | solution.py:1160
  259.0 3.3 collective-permute-start.46
  266.4 15.2 %expert_gradients.2 = (f32[8,3,2048,256]{3,2,1,0:T(8,128)}, f32[8,128]{1,0:T(8,128)S(1)}) custom-call(bf16[8,320,2048]{2,1,0:T(8,128)(2,1)} %get-tuple-element.109.refs_0_, bf16[8,320,2048]{2,1,0:T(8,128)(2,1)} %get-tuple-element.91.refs_0_.refs_1_, bf16[8,320,256]{2,1,0:T(8,128)(2,1)S(1)} %copy-done.6, bf16[8,320,256]{2,1,0:T(8,128)(2,1)S(1)} %copy-done.7, ...), custom_call_target="tpu_custom_call" | custom-call | flops 100000000 | bytes 300000 | tf_op jit(solution)/shard_map/expert_gradients/pallas_call | solution.py:1199
  281.6 3.9 collective-permute-done.45.refs_8_
  292.6 15.1 %expert_gradients.3 = (f32[8,3,2048,256]{3,2,1,0:T(8,128)}, f32[8,128]{1,0:T(8,128)S(1)}) custom-call(bf16[8,320,2048]{2,1,0:T(8,128)(2,1)} %get-tuple-element.109.refs_0_, bf16[8,320,2048]{2,1,0:T(8,128)(2,1)} %get-tuple-element.91.refs_0_.refs_1_, bf16[8,320,256]{2,1,0:T(8,128)(2,1)S(1)} %copy-done.6, ...), custom_call_target="tpu_custom_call", output_to_operand_aliasing={{0}: (5, {})} | custom-call | flops 100000000 | bytes 300000 | tf_op jit(solution)/shard_map/expert_gradients/pallas_call | solution.py:1199
  307.7 5.1 %collective-permute-done.48.refs_14_.refs_4_ = bf16[64,2176]{1,0:T(8,128)(2,1)S(1)} collective-permute-done((bf16[64,2176]{1,0:T(8,128)(2,1)S(1)}, bf16[64,2176]{1,0:T(8,128)(2,1)S(1)}, u32[]{:S(2)}, u32[]{:S(2)}) %collective-permute-start.48) | collective-permute-done | bytes 278560 | tf_op jit(solution)/shard_map/ppermute | solution.py:80
  313.7 12.9 %attend_backward.1 = (bf16[256,1536]{1,0:T(8,128)(2,1)}, bf16[64,4224]{1,0:T(8,128)(2,1)}, bf16[64,4224]{1,0:T(8,128)(2,1)}, bf16[64,4224]{1,0:T(8,128)(2,1)}, bf16[64,4224]{1,0:T(8,128)(2,1)}) custom-call(s32[2]{0:T(128)} %pad_add_fusion.refs_0_.pos_ref, bf16[256,2048]{1,0:T(8,128)(2,1)} %refs_1_.11, f32[256,128]{1,0:T(8,128)} %get-tuple-element.179.refs_2_.refs_7_, ...), custom_call_target="tpu_custom_call" | custom-call | flops 100000000 | bytes 300000 | tf_op jit(solution)/shard_map/attend_backward/pallas_call | solution.py:611
  332.2 4.1 projection_gradients.1
  338.0 12.7 %collective-permute-done.50.refs_6_.refs_11_ = bf16[64,4224]{1,0:T(8,128)(2,1)} collective-permute-done((bf16[64,4224]{1,0:T(8,128)(2,1)}, bf16[64,4224]{1,0:T(8,128)(2,1)}, u32[]{:S(2)}, u32[]{:S(2)}) %collective-permute-start.50) | collective-permute-done | bytes 540704 | tf_op jit(solution)/shard_map/ppermute | solution.py:80
  350.6 16.0 %collective-permute-done.51.refs_7_.refs_12_ = bf16[64,4224]{1,0:T(8,128)(2,1)} collective-permute-done((bf16[64,4224]{1,0:T(8,128)(2,1)}, bf16[64,4224]{1,0:T(8,128)(2,1)}, u32[]{:S(2)}, u32[]{:S(2)}) %collective-permute-start.51) | collective-permute-done | bytes 540704 | tf_op jit(solution)/shard_map/ppermute | solution.py:80
  366.6 4.1 last_rows.1.refs_2_
  373.0 3.2 output_gradients.1
  383.6 14.0 %collective-permute-done.60.refs_3_.new_y = bf16[2,128,1536]{2,1,0:T(8,128)(2,1)S(1)} collective-permute-done((bf16[2,128,1536]{2,1,0:T(8,128)(2,1)S(1)}, bf16[2,128,1536]{2,1,0:T(8,128)(2,1)S(1)}, u32[]{:S(2)}, u32[]{:S(2)}) %collective-permute-start.60) | collective-permute-done | bytes 786464 | tf_op jit(solution)/shard_map/ppermute | solution.py:80
  402.5 3.6 collective-permute-done.55.refs_2_.new_x
  409.2 3.8 collective-permute-done.61.end_x
  420.0 5.1 %all-gather.5.cloned.1.call-done.refs_0_ = bf16[256,4096]{1,0:T(8,128)(2,1)} async-done(((bf16[64,4096]{1,0:T(8,128)(2,1)}), bf16[256,4096]{1,0:T(8,128)(2,1)}) %all-gather.5.cloned.1.call-update) | async-done | bytes 2097168 | tf_op jit(solution)/shard_map/all_gather | solution.py:1356
  (314 shorter events, 135.5 us)
Async XLA Ops:
  7.2 116.8 %all-gather.3.cloned.1.call-start = ((), (), s32[]{:S(2)}) async-start(), calls=%async_computation.1 | async-start | bytes 10027008 | tf_op jit(solution)/shard_map/all_gather | solution.py:1297
  19.5 26.1 %collective-permute-start.1 = (bf16[128,2176]{1,0:T(8,128)(2,1)S(1)}, bf16[128,2176]{1,0:T(8,128)(2,1)}, u32[]{:S(2)}, u32[]{:S(2)}) collective-permute-start(bf16[128,2176]{1,0:T(8,128)(2,1)S(1)} %concatenate.20.refs_4_.refs_16_), channel_id=1, source_target_pairs={{0,8},{4,12},{8,0},{12,4},{16,24},{20,28},{24,16},{28,20},{1,9},{5... | collective-permute-start | bytes 1671176 | tf_op jit(solution)/shard_map/ppermute | solution.py:80
  20.0 25.6 %collective-permute-start.10 = (bf16[128,2176]{1,0:T(8,128)(2,1)S(1)}, bf16[128,2176]{1,0:T(8,128)(2,1)}, u32[]{:S(2)}, u32[]{:S(2)}) collective-permute-start(bf16[128,2176]{1,0:T(8,128)(2,1)S(1)} %concatenate.21.refs_12_.refs_24_), channel_id=1, source_target_pairs={{0,16},{4,20},{8,24},{12,28},{16,0},{20,4},{24,8},{28,12},{1,17},{... | collective-permute-start | bytes 1671176 | tf_op jit(solution)/shard_map/ppermute | solution.py:80
  30.8 25.2 %collective-permute-start.5 = (bf16[128,2176]{1,0:T(8,128)(2,1)}, bf16[128,2176]{1,0:T(8,128)(2,1)S(1)}, u32[]{:S(2)}, u32[]{:S(2)}) collective-permute-start(bf16[128,2176]{1,0:T(8,128)(2,1)} %collective-permute-done.3.refs_8_.refs_2_.refs_20_), channel_id=1, source_target_pairs={{0,8},{4,12},{8,0},{12,4},{16,24},{20,28},{24,16},{28,20},{1,9},{5... | collective-permute-start | bytes 1671176 | tf_op jit(solution)/shard_map/ppermute | solution.py:80
  33.7 22.3 %collective-permute-start.12 = (bf16[128,2176]{1,0:T(8,128)(2,1)}, bf16[128,2176]{1,0:T(8,128)(2,1)S(1)}, u32[]{:S(2)}, u32[]{:S(2)}) collective-permute-start(bf16[128,2176]{1,0:T(8,128)(2,1)} %collective-permute-done.8.refs_14_.refs_3_.refs_26_), channel_id=1, source_target_pairs={{0,16},{4,20},{8,24},{12,28},{16,0},{20,4},{24,8},{28,12},{1,17},{... | collective-permute-start | bytes 1671176 | tf_op jit(solution)/shard_map/ppermute | solution.py:80
  59.3 253.6 %reduce-scatter.2.cloned.1.call-start = ((), (), s32[]{:S(2)}) async-start(), calls=%async_computation.2 | async-start | bytes 9437184 | tf_op jit(solution)/shard_map/reduce_scatter | solution.py:1326
  79.7 21.5 %collective-permute-start.15 = (bf16[64,2048]{1,0:T(8,128)(2,1)}, bf16[64,2048]{1,0:T(8,128)(2,1)S(1)}, u32[]{:S(2)}, u32[]{:S(2)}) collective-permute-start(bf16[64,2048]{1,0:T(8,128)(2,1)} %get-tuple-element.85), channel_id=1, source_target_pairs={{0,2},{1,3},{2,0},{3,1},{4,6},{5,7},{6,4},{7,5},{8,10},{9,11},{10,... | collective-permute-start | bytes 786440 | tf_op jit(solution)/shard_map/ppermute | solution.py:80
  111.9 26.9 %collective-permute-start.19 = (bf16[64,2176]{1,0:T(8,128)(2,1)S(1)}, bf16[64,2176]{1,0:T(8,128)(2,1)S(1)}, u32[]{:S(2)}, u32[]{:S(2)}) collective-permute-start(bf16[64,2176]{1,0:T(8,128)(2,1)S(1)} %get-tuple-element.89.refs_0_.refs_6_), channel_id=1, source_target_pairs={{0,3},{1,2},{2,1},{3,0},{4,7},{5,6},{6,5},{7,4},{8,11},{9,10},{10,... | collective-permute-start | bytes 835592 | tf_op jit(solution)/shard_map/ppermute | solution.py:80
  114.3 24.5 %collective-permute-start.18 = (bf16[64,2176]{1,0:T(8,128)(2,1)S(1)}, bf16[64,2176]{1,0:T(8,128)(2,1)S(1)}, u32[]{:S(2)}, u32[]{:S(2)}) collective-permute-start(bf16[64,2176]{1,0:T(8,128)(2,1)S(1)} %get-tuple-element.89.refs_0_.refs_6_), channel_id=1, source_target_pairs={{0,2},{1,3},{2,0},{3,1},{4,6},{5,7},{6,4},{7,5},{8,10},{9,11},{10,... | collective-permute-start | bytes 835592 | tf_op jit(solution)/shard_map/ppermute | solution.py:80
  121.5 20.5 %collective-permute-start.23 = (bf16[128,2176]{1,0:T(8,128)(2,1)}, bf16[128,2176]{1,0:T(8,128)(2,1)S(1)}, u32[]{:S(2)}, u32[]{:S(2)}) collective-permute-start(bf16[128,2176]{1,0:T(8,128)(2,1)} %joins.5.refs_2_.refs_0_), channel_id=1, source_target_pairs={{0,16},{4,20},{8,24},{12,28},{16,0},{20,4},{24,8},{28,12},{1,17},{... | collective-permute-start | bytes 1671176 | tf_op jit(solution)/shard_map/ppermute | solution.py:80
  122.5 21.2 %collective-permute-start.21 = (bf16[128,2176]{1,0:T(8,128)(2,1)}, bf16[128,2176]{1,0:T(8,128)(2,1)S(1)}, u32[]{:S(2)}, u32[]{:S(2)}) collective-permute-start(bf16[128,2176]{1,0:T(8,128)(2,1)} %joins.5.refs_2_.refs_0_), channel_id=1, source_target_pairs={{0,8},{4,12},{8,0},{12,4},{16,24},{20,28},{24,16},{28,20},{1,9},{5... | collective-permute-start | bytes 1671176 | tf_op jit(solution)/shard_map/ppermute | solution.py:80
  142.0 22.9 %collective-permute-start.25 = (bf16[128,2176]{1,0:T(8,128)(2,1)S(1)}, bf16[128,2176]{1,0:T(8,128)(2,1)}, u32[]{:S(2)}, u32[]{:S(2)}) collective-permute-start(bf16[128,2176]{1,0:T(8,128)(2,1)S(1)} %collective-permute-done.23.refs_4_), channel_id=1, source_target_pairs={{0,8},{4,12},{8,0},{12,4},{16,24},{20,28},{24,16},{28,20},{1,9},{5... | collective-permute-start | bytes 1671176 | tf_op jit(solution)/shard_map/ppermute | solution.py:80
  143.6 21.4 %collective-permute-start.24 = (bf16[128,2176]{1,0:T(8,128)(2,1)S(1)}, bf16[128,2176]{1,0:T(8,128)(2,1)}, u32[]{:S(2)}, u32[]{:S(2)}) collective-permute-start(bf16[128,2176]{1,0:T(8,128)(2,1)S(1)} %collective-permute-done.23.refs_4_), channel_id=1, source_target_pairs={{0,4},{4,0},{8,12},{12,8},{16,20},{20,16},{24,28},{28,24},{1,5},{5... | collective-permute-start | bytes 1671176 | tf_op jit(solution)/shard_map/ppermute | solution.py:80
  143.7 21.7 %collective-permute-start.22 = (bf16[128,2176]{1,0:T(8,128)(2,1)S(1)}, bf16[128,2176]{1,0:T(8,128)(2,1)}, u32[]{:S(2)}, u32[]{:S(2)}) collective-permute-start(bf16[128,2176]{1,0:T(8,128)(2,1)S(1)} %collective-permute-done.21.refs_2_), channel_id=1, source_target_pairs={{0,4},{4,0},{8,12},{12,8},{16,20},{20,16},{24,28},{28,24},{1,5},{5... | collective-permute-start | bytes 1671176 | tf_op jit(solution)/shard_map/ppermute | solution.py:80
  160.3 19.9 %collective-permute-start.32 = (bf16[128,2176]{1,0:T(8,128)(2,1)}, bf16[128,2176]{1,0:T(8,128)(2,1)S(1)}, u32[]{:S(2)}, u32[]{:S(2)}) collective-permute-start(bf16[128,2176]{1,0:T(8,128)(2,1)} %joins.7), channel_id=1, source_target_pairs={{0,16},{4,20},{8,24},{12,28},{16,0},{20,4},{24,8},{28,12},{1,17},{... | collective-permute-start | bytes 1671176 | tf_op jit(solution)/shard_map/ppermute | solution.py:80
  221.7 19.6 %collective-permute-start.39 = (bf16[2,64,2176]{2,1,0:T(8,128)(2,1)}, bf16[2,64,2176]{2,1,0:T(8,128)(2,1)}, u32[]{:S(2)}, u32[]{:S(2)}) collective-permute-start(bf16[2,64,2176]{2,1,0:T(8,128)(2,1)} %get-tuple-element.99), channel_id=1, source_target_pairs={{0,16},{4,20},{8,24},{12,28},{16,0},{20,4},{24,8},{28,12},{1,17},{... | collective-permute-start | bytes 1671176 | tf_op jit(solution)/shard_map/ppermute | solution.py:80
  225.8 23.6 %collective-permute-start.36 = (bf16[2,64,2176]{2,1,0:T(8,128)(2,1)}, bf16[2,64,2176]{2,1,0:T(8,128)(2,1)}, u32[]{:S(2)}, u32[]{:S(2)}) collective-permute-start(bf16[2,64,2176]{2,1,0:T(8,128)(2,1)} %get-tuple-element.95), channel_id=1, source_target_pairs={{0,16},{4,20},{8,24},{12,28},{16,0},{20,4},{24,8},{28,12},{1,17},{... | collective-permute-start | bytes 1671176 | tf_op jit(solution)/shard_map/ppermute | solution.py:80
  226.8 23.8 %collective-permute-start.35 = (bf16[2,64,2176]{2,1,0:T(8,128)(2,1)}, bf16[2,64,2176]{2,1,0:T(8,128)(2,1)}, u32[]{:S(2)}, u32[]{:S(2)}) collective-permute-start(bf16[2,64,2176]{2,1,0:T(8,128)(2,1)} %get-tuple-element.94.refs_5_), channel_id=1, source_target_pairs={{0,8},{4,12},{8,0},{12,4},{16,24},{20,28},{24,16},{28,20},{1,9},{5... | collective-permute-start | bytes 1671176 | tf_op jit(solution)/shard_map/ppermute | solution.py:80
  241.2 183.9 %all-gather.5.cloned.1.call-start = ((), (), s32[]{:S(2)}) async-start(), calls=%async_computation.3 | async-start | bytes 2621440 | tf_op jit(solution)/shard_map/all_gather | solution.py:1356
  259.0 22.6 %collective-permute-start.46 = (bf16[64,2176]{1,0:T(8,128)(2,1)S(1)}, bf16[64,2176]{1,0:T(8,128)(2,1)S(1)}, u32[]{:S(2)}, u32[]{:S(2)}) collective-permute-start(bf16[64,2176]{1,0:T(8,128)(2,1)S(1)} %get-tuple-element.108), channel_id=1, source_target_pairs={{0,3},{1,2},{2,1},{3,0},{4,7},{5,6},{6,5},{7,4},{8,11},{9,10},{10,... | collective-permute-start | bytes 835592 | tf_op jit(solution)/shard_map/ppermute | solution.py:80
  262.3 23.2 %collective-permute-start.45 = (bf16[64,2176]{1,0:T(8,128)(2,1)S(1)}, bf16[64,2176]{1,0:T(8,128)(2,1)S(1)}, u32[]{:S(2)}, u32[]{:S(2)}) collective-permute-start(bf16[64,2176]{1,0:T(8,128)(2,1)S(1)} %get-tuple-element.105.refs_6_), channel_id=1, source_target_pairs={{0,2},{1,3},{2,0},{3,1},{4,6},{5,7},{6,4},{7,5},{8,10},{9,11},{10,... | collective-permute-start | bytes 835592 | tf_op jit(solution)/shard_map/ppermute | solution.py:80
  265.5 20.0 %collective-permute-start.44 = (bf16[64,2176]{1,0:T(8,128)(2,1)S(1)}, bf16[64,2176]{1,0:T(8,128)(2,1)S(1)}, u32[]{:S(2)}, u32[]{:S(2)}) collective-permute-start(bf16[64,2176]{1,0:T(8,128)(2,1)S(1)} %get-tuple-element.107), channel_id=1, source_target_pairs={{0,1},{1,0},{2,3},{3,2},{4,5},{5,4},{6,7},{7,6},{8,9},{9,8},{10,11... | collective-permute-start | bytes 835592 | tf_op jit(solution)/shard_map/ppermute | solution.py:80
  290.6 22.2 %collective-permute-start.48 = (bf16[64,2176]{1,0:T(8,128)(2,1)S(1)}, bf16[64,2176]{1,0:T(8,128)(2,1)S(1)}, u32[]{:S(2)}, u32[]{:S(2)}) collective-permute-start(bf16[64,2176]{1,0:T(8,128)(2,1)S(1)} %get-tuple-element.120.refs_6_.refs_12_.refs_2_), channel_id=1, source_target_pairs={{0,2},{1,3},{2,0},{3,1},{4,6},{5,7},{6,4},{7,5},{8,10},{9,11},{10,... | collective-permute-start | bytes 835592 | tf_op jit(solution)/shard_map/ppermute | solution.py:80
  290.6 22.2 %collective-permute-start.47 = (bf16[64,2176]{1,0:T(8,128)(2,1)S(1)}, bf16[64,2176]{1,0:T(8,128)(2,1)S(1)}, u32[]{:S(2)}, u32[]{:S(2)}) collective-permute-start(bf16[64,2176]{1,0:T(8,128)(2,1)S(1)} %get-tuple-element.120.refs_6_.refs_12_.refs_2_), channel_id=1, source_target_pairs={{0,1},{1,0},{2,3},{3,2},{4,5},{5,4},{6,7},{7,6},{8,9},{9,8},{10,11... | collective-permute-start | bytes 835592 | tf_op jit(solution)/shard_map/ppermute | solution.py:80
  326.6 24.0 %collective-permute-start.50 = (bf16[64,4224]{1,0:T(8,128)(2,1)}, bf16[64,4224]{1,0:T(8,128)(2,1)}, u32[]{:S(2)}, u32[]{:S(2)}) collective-permute-start(bf16[64,4224]{1,0:T(8,128)(2,1)} %get-tuple-element.124), channel_id=1, source_target_pairs={{0,1},{1,0},{2,3},{3,2},{4,5},{5,4},{6,7},{7,6},{8,9},{9,8},{10,11... | collective-permute-start | bytes 1622024 | tf_op jit(solution)/shard_map/ppermute | solution.py:80
  327.0 39.6 %collective-permute-start.51 = (bf16[64,4224]{1,0:T(8,128)(2,1)}, bf16[64,4224]{1,0:T(8,128)(2,1)}, u32[]{:S(2)}, u32[]{:S(2)}) collective-permute-start(bf16[64,4224]{1,0:T(8,128)(2,1)} %get-tuple-element.125), channel_id=1, source_target_pairs={{0,2},{1,3},{2,0},{3,1},{4,6},{5,7},{6,4},{7,5},{8,10},{9,11},{10,... | collective-permute-start | bytes 1622024 | tf_op jit(solution)/shard_map/ppermute | solution.py:80
  329.5 37.1 %collective-permute-start.52 = (bf16[64,4224]{1,0:T(8,128)(2,1)}, bf16[64,4224]{1,0:T(8,128)(2,1)}, u32[]{:S(2)}, u32[]{:S(2)}) collective-permute-start(bf16[64,4224]{1,0:T(8,128)(2,1)} %get-tuple-element.126), channel_id=1, source_target_pairs={{0,3},{1,2},{2,1},{3,0},{4,7},{5,6},{6,5},{7,4},{8,11},{9,10},{10,... | collective-permute-start | bytes 1622024 | tf_op jit(solution)/shard_map/ppermute | solution.py:80
  338.0 32.8 %collective-permute-start.53 = (bf16[4,256,1536]{2,1,0:T(8,128)(2,1)}, bf16[4,256,1536]{2,1,0:T(8,128)(2,1)S(1)}, u32[]{:S(2)}, u32[]{:S(2)}) collective-permute-start(bf16[4,256,1536]{2,1,0:T(8,128)(2,1)} %get-tuple-element.131), channel_id=1, source_target_pairs={{0,4},{4,0},{8,12},{12,8},{16,20},{20,16},{24,28},{28,24},{1,5},{5... | collective-permute-start | bytes 9437192 | tf_op jit(solution)/shard_map/ppermute | solution.py:80
  377.3 20.3 %collective-permute-start.60 = (bf16[2,128,1536]{2,1,0:T(8,128)(2,1)S(1)}, bf16[2,128,1536]{2,1,0:T(8,128)(2,1)S(1)}, u32[]{:S(2)}, u32[]{:S(2)}) collective-permute-start(bf16[2,128,1536]{2,1,0:T(8,128)(2,1)S(1)} %get-tuple-element.140), channel_id=1, source_target_pairs={{0,16},{4,20},{8,24},{12,28},{16,0},{20,4},{24,8},{28,12},{1,17},{... | collective-permute-start | bytes 2359304 | tf_op jit(solution)/shard_map/ppermute | solution.py:80
  378.6 20.4 %collective-permute-start.59 = (bf16[2,128,1536]{2,1,0:T(8,128)(2,1)S(1)}, bf16[2,128,1536]{2,1,0:T(8,128)(2,1)S(1)}, u32[]{:S(2)}, u32[]{:S(2)}) collective-permute-start(bf16[2,128,1536]{2,1,0:T(8,128)(2,1)S(1)} %get-tuple-element.132.refs_14_), channel_id=1, source_target_pairs={{0,8},{4,12},{8,0},{12,4},{16,24},{20,28},{24,16},{28,20},{1,9},{5... | collective-permute-start | bytes 2359304 | tf_op jit(solution)/shard_map/ppermute | solution.py:80
  381.5 24.5 %collective-permute-start.55 = (bf16[2,128,640]{2,1,0:T(8,128)(2,1)S(1)}, bf16[2,128,640]{2,1,0:T(8,128)(2,1)S(1)}, u32[]{:S(2)}, u32[]{:S(2)}) collective-permute-start(bf16[2,128,640]{2,1,0:T(8,128)(2,1)S(1)} %get-tuple-element.135), channel_id=1, source_target_pairs={{0,8},{4,12},{8,0},{12,4},{16,24},{20,28},{24,16},{28,20},{1,9},{5... | collective-permute-start | bytes 983048 | tf_op jit(solution)/shard_map/ppermute | solution.py:80
  383.0 23.0 %collective-permute-start.56 = (bf16[2,128,640]{2,1,0:T(8,128)(2,1)S(1)}, bf16[2,128,640]{2,1,0:T(8,128)(2,1)S(1)}, u32[]{:S(2)}, u32[]{:S(2)}) collective-permute-start(bf16[2,128,640]{2,1,0:T(8,128)(2,1)S(1)} %get-tuple-element.136), channel_id=1, source_target_pairs={{0,16},{4,20},{8,24},{12,28},{16,0},{20,4},{24,8},{28,12},{1,17},{... | collective-permute-start | bytes 983048 | tf_op jit(solution)/shard_map/ppermute | solution.py:80
  (107 other events, 889.6 us)
Sparse Core Ops, SparseCore 0:
  59.4 56.8 all-gather.2
  241.4 71.0 reduce-scatter.1
  370.8 54.2 all-gather.4
where the time goes:
time: 441 us; the launch traced here: 434 us
  Pallas kernels  170 us (39%)
  waiting for transfers between devices  160 us (36%)
  starting transfers between devices  59.8 us (14%)
  local copies, waits for them, and re-layouts  26.6 us (6%)
  between operations  15 us (3%)
    ppermute x63, waiting for transfers between devices, swap(): return lax.ppermute(block, axis, [(i, i ^ step) for i in range(size)])  155 us
    ppermute x63, starting transfers between devices, swap(): return lax.ppermute(block, axis, [(i, i ^ step) for i in range(size)])  59.2 us
    pallas_call x1, Pallas kernels, run_experts(): pl.pallas_call(kernel, out_shape=[shape((number, filled, D), BF16), shape...  31.6 us
    pallas_call x2, Pallas kernels, expert_gradients(): pl.pallas_call(without(kernel, 5, len(before) + len(deps)), out_shape=[sh...  30.3 us
    unnamed x149, local copies, waits for them, and re-layouts  16.5 us
    pallas_call x1, Pallas kernels, route_cotangent(): pl.pallas_call(without(kernel, 1 + count, len(deps)), out_shape=[shape((n...  14.7 us
    pallas_call x1, Pallas kernels, attend_backward(): pl.pallas_call(without(kernel, 12 + nt + count, len(deps)), out_shape=[sh...  12.9 us
    pallas_call x1, Pallas kernels, expert_outputs(): pl.pallas_call(without(kernel, 4, len(deps)), out_shape=shape((nf, length...  12.9 us
  transfers between devices with their start and end apart: 66, of which 36 were waited for; matrix products, arithmetic and copies ran while one was open for 2% of the time, Pallas kernels for 28%

commit v1 on v0

--- a/solution.py
+++ b/solution.py
@@ -216,15 +216,16 @@
     return found
 
 
-def start_fetch(pieces, refs, place, sems, own=None):
+def start_fetch(pieces, refs, place, sems, own=None, columns=None):
     arrays = arrays_of(pieces)
+    span = slice(None) if columns is None else pl.ds(*columns)
     copies = []
     for k, (index, row, part, at, rows) in enumerate(pieces):
         ref = next(ref for other, ref in zip(arrays, refs) if other is part)
         if at is None:
             at = pl.multiple_of((own ^ index) * rows, 16)
         copy = pltpu.make_async_copy(
-            ref.at[pl.ds(at, rows), :], place(index, row, rows), sems.at[k]
+            ref.at[pl.ds(at, rows), span], place(index, row, rows), sems.at[k]
         )
         copy.start()
         copies.append(copy)
@@ -462,14 +463,20 @@
         part_refs, (w, out, sems) = refs[9 : 9 + nt], refs[9 + nt :]
         f, t = pos_ref[0], pos_ref[1]
 
-        def place(index, row, number):
+        def place(index, row, number, span):
             start = pl.multiple_of((f ^ index) * block + row, 16)
-            return w.at[pl.ds(start, number), :]
-
-        copies = start_fetch(pieces, piece_refs, place, sems)
+            return w.at[pl.ds(start, number), pl.ds(*span)]
+
+        spans = ((4 * width, SIDE), (0, 3 * width), (3 * width, width))
+        side, copies, later = [
+            start_fetch(
+                pieces, piece_refs, functools.partial(place, span=span), sems.at[k], columns=span
+            )
+            for k, span in enumerate(spans)
+        ]
         x = x_ref[...].astype(F32)
         normed = x * rms_inverse(x)
-        for copy in copies:
+        for copy in side:
             copy.wait()
         side_ref[...] = w[:, 4 * width :]
         turned = jnp.transpose(w[:, 4 * width :].astype(F32))
@@ -481,6 +488,8 @@
         head_gain_ref[...] = head_gains
         n1 = (normed * turned[EXPERTS : EXPERTS + 1]).astype(BF16)
         n1_ref[...] = n1
+        for copy in copies:
+            copy.wait()
         raw = dot(n1, w[:, : 3 * width])
         qk_ref[...] = raw[:, : 2 * width]
         v_ref[...] = raw[:, 2 * width :].astype(BF16)
@@ -499,6 +508,8 @@
             probs = shifted / jnp.sum(shifted, axis=-1, keepdims=True)
             prob_ref[h] = probs
             att_ref[:, span] = dot(probs.astype(BF16), v_ref[:, span]).astype(BF16)
+        for copy in later:
+            copy.wait()
         out[...] = dot_nt(att_ref[...], w[:, 3 * width : 4 * width]).astype(BF16)
         for d in range(nt):
             start = pl.multiple_of((t ^ d) * rows, 16)
@@ -523,12 +534,12 @@
         scratch_shapes=[
             pltpu.VMEM((D, columns), BF16),
             pltpu.VMEM((length, D), BF16),
-            pltpu.SemaphoreType.DMA((len(pieces),)),
+            pltpu.SemaphoreType.DMA((3, len(pieces))),
         ],
         compiler_params=params(60),
         cost_estimate=cost(5),
         name="attend_forward",
-    )(pos, tokens, cosine, sine, *arrays, *deps)
+    )(pos, tokens, cosine, sine, *in_hbm(arrays), *deps)
     return results[:9], results[9:]
 
 
@@ -551,11 +562,17 @@
         part_refs, (w, out, db_ref, sems) = refs[1 : 1 + nt], refs[1 + nt :]
         f, t = pos_ref[0], pos_ref[1]
 
-        def place(index, row, number):
+        def place(index, row, number, span):
             start = pl.multiple_of((f ^ index) * block + row, 16)
-            return w.at[pl.ds(start, number), :]
-
-        copies = start_fetch(pieces, piece_refs, place, sems)
+            return w.at[pl.ds(start, number), pl.ds(*span)]
+
+        spans = ((3 * width, width), (0, 3 * width))
+        copies, later = [
+            start_fetch(
+                pieces, piece_refs, functools.partial(place, span=span), sems.at[k], columns=span
+            )
+            for k, span in enumerate(spans)
+        ]
         for d in range(nt):
             start = pl.multiple_of((t ^ d) * rows, 16)
             db_ref[pl.ds(start, rows), :] = grad_refs[d][:, :D]
@@ -590,6 +607,8 @@
                 dqkv_ref[:, span_w] = norm_backward(
                     raw, inverse, head_gains[2 + which : 3 + which], grads
                 ).astype(BF16)
+        for copy in later:
+            copy.wait()
         grad_normed = dot_nt(dqkv_ref[...], w[:, : 3 * width])
         out[...] = grad_normed.astype(BF16)
         x = x_ref[...].astype(F32)
@@ -620,14 +639,14 @@
             pltpu.VMEM((D, columns), BF16),
             pltpu.VMEM((length, D), BF16),
             pltpu.VMEM((length, D), BF16),
-            pltpu.SemaphoreType.DMA((len(pieces),)),
+            pltpu.SemaphoreType.DMA((2, len(pieces))),
         ],
         compiler_params=params(60),
         cost_estimate=cost(0.1),
         name="attend_backward",
     )(
         pos, tokens, cosine, sine, qk, rot, values, probs, gains, head_gains, ffn_row, layer_sum,
-        *grad_rows, *arrays, *deps,
+        *grad_rows, *in_hbm(arrays), *deps,
     )
     return results[0], results[1:]
 
@@ -723,12 +742,32 @@
     rows = tokens.shape[0] // nt
     top = routes.shape[1]
 
-    def kernel(pos_ref, x_ref, route_ref, gain_ref, side_ref, *refs):
-        part_refs, (h_ref, next_ref, gate_ref) = refs[:nt], refs[nt:]
-        h = x_ref[...].astype(F32)
+    def kernel(pos_ref, route_all, x_all, gain_all, side_all, first_all, *refs):
+        part_refs, refs = refs[: nt - 1], refs[nt - 1 :]
+        h_ref, next_ref, gate_ref, x_ref, gain_ref, side_ref, first_ref, sems = refs
+        mine = pl.ds(pl.multiple_of(pos_ref[1] * rows, 16), rows)
+        copies = [
+            pltpu.make_async_copy(source, target, sems.at[k])
+            for k, (source, target) in enumerate(
+                (
+                    (x_all.at[mine, :], x_ref),
+                    (first_all, first_ref),
+                    (gain_all, gain_ref),
+                    (side_all, side_ref),
+                )
+            )
+        ]
+        for copy in copies:
+            copy.start()
+        route_ref = route_all.at[mine, :]
+        copies[0].wait()
+        copies[1].wait()
+        h = x_ref[...].astype(F32) + first_ref[...].astype(F32)
         for ref in part_refs:
             h = h + ref[...].astype(F32)
         h_ref[...] = h
+        copies[2].wait()
+        copies[3].wait()
         n2 = (h * rms_inverse(h) * gain_ref[1:2]).astype(BF16)
         next_ref[:, :D] = n2
         logits = dot(n2, side_ref[...])
@@ -744,32 +783,25 @@
         rest = (gates - first).astype(BF16).astype(F32)
         next_ref[:, D:] = (first + pltpu.roll(rest, EXPERTS, 1)).astype(BF16)
 
-    whole = lambda i, pos: (0, 0)
-    mine = lambda i, pos: (pos[1], 0)
     return pl.pallas_call(
         without(kernel, 5 + nt, len(deps)),
         out_shape=[shape((rows, D), F32), shape((rows, D + SIDE), BF16), shape((rows, SIDE), F32)],
-        grid_spec=pltpu.PrefetchScalarGridSpec(
-            num_scalar_prefetch=1,
-            grid=(1,),
-            in_specs=[
-                pl.BlockSpec((rows, D), mine),
-                pl.BlockSpec((rows, top), mine),
-                pl.BlockSpec((8, D), whole),
-                pl.BlockSpec((D, SIDE), whole),
-            ]
-            + [pl.BlockSpec((rows, D), whole)] * nt
-            + [HBM] * len(deps),
-            out_specs=[
-                pl.BlockSpec((rows, D), whole),
-                pl.BlockSpec((rows, D + SIDE), whole),
-                pl.BlockSpec((rows, SIDE), whole),
-            ],
-        ),
-        compiler_params=params(),
+        in_specs=[SMEM, VMEM] + [HBM] * 4 + [VMEM] * (nt - 1) + [HBM] * len(deps),
+        out_specs=[VMEM] * 3,
+        scratch_shapes=[
+            pltpu.VMEM((rows, D), BF16),
+            pltpu.VMEM((8, D), F32),
+            pltpu.VMEM((D, SIDE), BF16),
+            pltpu.VMEM((rows, D), BF16),
+            pltpu.SemaphoreType.DMA((4,)),
+        ],
+        compiler_params=params(60),
         cost_estimate=cost(100),
         name="norm_and_route",
-    )(pos, tokens, routes, gains, side, *parts, *deps)
+    )(
+        pos, routes, *in_hbm([tokens, gains, side, parts[0]]),
+        *[near_core(part) for part in parts[1:]], *in_hbm(deps),
+    )
 
 
 def norm_back(pos, cotangent, parts, h, gates, gains, side, nt, deps=()):
@@ -828,11 +860,29 @@
     rows = dh.shape[0]
     columns = parts[0].shape[1]
 
-    def kernel(pos_ref, x_ref, dh_ref, h_ref, gain_ref, *refs):
-        part_refs, out_ref = refs[:nt], refs[nt]
-        total = part_refs[0][:, :D].astype(F32)
-        layer = h_ref[...] + part_refs[0][:, columns - D :].astype(F32)
-        for ref in part_refs[1:]:
+    def kernel(pos_ref, x_all, dh_all, h_all, gain_all, first_all, *refs):
+        part_refs, refs = refs[: nt - 1], refs[nt - 1 :]
+        out_ref, x_ref, dh_ref, h_ref, gain_ref, first_ref, sems = refs
+        mine = pl.ds(pl.multiple_of(pos_ref[1] * rows, 16), rows)
+        copies = [
+            pltpu.make_async_copy(source, target, sems.at[k])
+            for k, (source, target) in enumerate(
+                (
+                    (first_all, first_ref),
+                    (x_all.at[mine, :], x_ref),
+                    (gain_all, gain_ref),
+                    (h_all, h_ref),
+                    (dh_all, dh_ref),
+                )
+            )
+        ]
+        for copy in copies:
+            copy.start()
+        for copy in copies:
+            copy.wait()
+        total = first_ref[:, :D].astype(F32)
+        layer = h_ref[...] + first_ref[:, columns - D :].astype(F32)
+        for ref in part_refs:
             total = total + ref[:, :D].astype(F32)
             layer = layer + ref[:, columns - D :].astype(F32)
         x = x_ref[...].astype(F32)
@@ -841,27 +891,26 @@
         ).astype(BF16)
         out_ref[:, D:] = layer.astype(BF16)
 
-    whole = lambda i, pos: (0, 0)
     return pl.pallas_call(
         without(kernel, 5 + nt, len(deps)),
         out_shape=shape((rows, 2 * D), BF16),
-        grid_spec=pltpu.PrefetchScalarGridSpec(
-            num_scalar_prefetch=1,
-            grid=(1,),
-            in_specs=[
-                pl.BlockSpec((rows, D), lambda i, pos: (pos[1], 0)),
-                pl.BlockSpec((rows, D), whole),
-                pl.BlockSpec((rows, D), whole),
-                pl.BlockSpec((8, D), whole),
-            ]
-            + [pl.BlockSpec((rows, columns), whole)] * nt
-            + [HBM] * len(deps),
-            out_specs=pl.BlockSpec((rows, 2 * D), whole),
-        ),
+        in_specs=[SMEM] + [HBM] * 5 + [VMEM] * (nt - 1) + [HBM] * len(deps),
+        out_specs=VMEM,
+        scratch_shapes=[
+            pltpu.VMEM((rows, D), BF16),
+            pltpu.VMEM((rows, D), F32),
+            pltpu.VMEM((rows, D), F32),
+            pltpu.VMEM((8, D), F32),
+            pltpu.VMEM((rows, columns), BF16),
+            pltpu.SemaphoreType.DMA((5,)),
+        ],
         compiler_params=params(60),
         cost_estimate=cost(100),
         name="last_rows",
-    )(pos, tokens, dh, h, gains, *parts, *deps)
+    )(
+        pos, *in_hbm([tokens, dh, h, gains, parts[0]]),
+        *[near_core(part) for part in parts[1:]], *in_hbm(deps),
+    )
 
 
 def place_rows(pos, parts):
@@ -975,7 +1024,7 @@
         compiler_params=params(60),
         cost_estimate=cost(0.1),
         name="route_cotangent",
-    )(pos, *arrays, *deps)
+    )(pos, *in_hbm(arrays), *deps)
 
 
 def down_back(grad_rows, weights, deps=()):
@@ -1125,7 +1174,7 @@
         compiler_params=params(60),
         cost_estimate=cost(5),
         name="run_experts",
-    )(pos, slot_table, down, weights, weights, *arrays)
+    )(pos, slot_table, down, weights, weights, *in_hbm(arrays))
 
 
 def expert_outputs(pos, slot_table, hidden, weights, nt, deps=()):
@@ -1287,10 +1336,7 @@
         weights = gather_two(packed, weights_near, nf)
         wide_cot = join(
             [wide_cot],
-            weights_near[0]
-            + weights_near[1]
-            + [w[2] for w in weights if w[0] == nf - 2]
-            + [cosine, sine],
+            [w[2] for w in weights if w[0] not in (0, nf - 1)] + [cosine, sine],
         )
     else:
         weights = gather_rest(packed, gather_near(packed, nf), nf)

time: 441 us -> 438 us (level)
  waiting for transfers between devices: 160 us -> 155 us
    unnamed x149 -> x135, local copies, waits for them, and re-layouts: 16.5 us -> 14.4 us
  transfers between devices with their start and end apart: 66 -> 66, of which waited for: 36 -> 29; matrix products, arithmetic and copies ran while one was open for 2% -> 2% of each run, Pallas kernels for 28% -> 29%
where the time goes in v1:
time: 438 us; the launch traced here: 431 us
  Pallas kernels  174 us (40%)
  waiting for transfers between devices  155 us (35%)
  starting transfers between devices  57.6 us (13%)
  local copies, waits for them, and re-layouts  25.9 us (6%)
  between operations  15.2 us (3%)
    ppermute x63, waiting for transfers between devices, swap(): return lax.ppermute(block, axis, [(i, i ^ step) for i in range(size)])  151 us
    ppermute x63, starting transfers between devices, swap(): return lax.ppermute(block, axis, [(i, i ^ step) for i in range(size)])  57 us
    pallas_call x1, Pallas kernels, run_experts(): pl.pallas_call(kernel, out_shape=[shape((number, filled, D), BF16), shape...  31.6 us
    pallas_call x2, Pallas kernels, expert_gradients(): pl.pallas_call(without(kernel, 5, len(before) + len(deps)), out_shape=[sh...  30.3 us
    pallas_call x1, Pallas kernels, route_cotangent(): pl.pallas_call(without(kernel, 1 + count, len(deps)), out_shape=[shape((n...  14.7 us
    unnamed x135, local copies, waits for them, and re-layouts  14.4 us
    pallas_call x1, Pallas kernels, expert_outputs(): pl.pallas_call(without(kernel, 4, len(deps)), out_shape=shape((nf, length...  12.9 us
    pallas_call x1, Pallas kernels, attend_backward(): pl.pallas_call(without(kernel, 12 + nt + count, len(deps)), out_shape=[sh...  11.2 us
  transfers between devices with their start and end apart: 66, of which 29 were waited for; matrix products, arithmetic and copies ran while one was open for 2% of the time, Pallas kernels for 29%

profile of v1, /device:TPU:0, one launch (start us, length us, event | category | flops | bytes accessed | tf_op | source)
XLA Modules:
  0.0 430.6 jit_solution(9550120378920148713)
XLA Ops:
  21.2 10.3 %collective-permute-done.3.refs_8_.refs_4_.refs_20_ = bf16[128,2176]{1,0:T(8,128)(2,1)S(1)} collective-permute-done((bf16[128,2176]{1,0:T(8,128)(2,1)}, bf16[128,2176]{1,0:T(8,128)(2,1)S(1)}, u32[]{:S(2)}, u32[]{:S(2)}) %collective-permute-start.3) | collective-permute-done | bytes 557088 | tf_op jit(solution)/shard_map/ppermute | solution.py:80
  36.4 9.3 %collective-permute-done.8.refs_14_.refs_8_.refs_26_ = bf16[128,2176]{1,0:T(8,128)(2,1)} collective-permute-done((bf16[128,2176]{1,0:T(8,128)(2,1)}, bf16[128,2176]{1,0:T(8,128)(2,1)}, u32[]{:S(2)}, u32[]{:S(2)}) %collective-permute-start.8) | collective-permute-done | bytes 557088 | tf_op jit(solution)/shard_map/ppermute | solution.py:80
  46.1 9.9 %collective-permute-done.5.refs_10_.refs_6_.refs_22_ = bf16[128,2176]{1,0:T(8,128)(2,1)} collective-permute-done((bf16[128,2176]{1,0:T(8,128)(2,1)S(1)}, bf16[128,2176]{1,0:T(8,128)(2,1)}, u32[]{:S(2)}, u32[]{:S(2)}) %collective-permute-start.5) | collective-permute-done | bytes 557088 | tf_op jit(solution)/shard_map/ppermute | solution.py:80
  67.1 10.7 %attend_forward.1 = (bf16[256,2048]{1,0:T(8,128)(2,1)}, f32[256,1024]{1,0:T(8,128)}, bf16[256,1024]{1,0:T(8,128)(2,1)}, bf16[256,512]{1,0:T(8,128)(2,1)}, f32[4,...) custom-call(s32[2]{0:T(128)} %pad_add_fusion.refs_0_.pos_ref, ...), custom_call_target="tpu_custom_call" | custom-call | flops 5000000000 | bytes 15000000 | tf_op jit(solution)/shard_map/attend_forward/pallas_call | solution.py:518
  83.1 8.8 %collective-permute-done.14.refs_6_ = bf16[64,2048]{1,0:T(8,128)(2,1)S(1)} collective-permute-done((bf16[64,2048]{1,0:T(8,128)(2,1)}, bf16[64,2048]{1,0:T(8,128)(2,1)S(1)}, u32[]{:S(2)}, u32[]{:S(2)}) %collective-permute-start.14) | collective-permute-done | bytes 262176 | tf_op jit(solution)/shard_map/ppermute | solution.py:80
  91.9 9.1 %collective-permute-done.15.refs_7_ = bf16[64,2048]{1,0:T(8,128)(2,1)S(1)} collective-permute-done((bf16[64,2048]{1,0:T(8,128)(2,1)}, bf16[64,2048]{1,0:T(8,128)(2,1)S(1)}, u32[]{:S(2)}, u32[]{:S(2)}) %collective-permute-start.15) | collective-permute-done | bytes 262176 | tf_op jit(solution)/shard_map/ppermute | solution.py:80
  100.9 3.5 norm_and_route.1
  104.4 5.5 %collective-permute-start.17 = (bf16[64,2176]{1,0:T(8,128)(2,1)}, bf16[64,2176]{1,0:T(8,128)(2,1)S(1)}, u32[]{:S(2)}, u32[]{:S(2)}) collective-permute-start(bf16[64,2176]{1,0:T(8,128)(2,1)} %get-tuple-element.89.refs_0_.refs_6_), channel_id=1, source_target_pairs={{0,1},{1,0},{2,3},{3,2},{4,5},{5,4},{6,7},{7,6},{8,9},{9,8},{10,11... | collective-permute-start | bytes 835592 | tf_op jit(solution)/shard_map/ppermute | solution.py:80
  112.4 4.9 %collective-permute-done.17.refs_1_.refs_7_ = bf16[64,2176]{1,0:T(8,128)(2,1)S(1)} collective-permute-done((bf16[64,2176]{1,0:T(8,128)(2,1)}, bf16[64,2176]{1,0:T(8,128)(2,1)S(1)}, u32[]{:S(2)}, u32[]{:S(2)}) %collective-permute-start.17) | collective-permute-done | bytes 278560 | tf_op jit(solution)/shard_map/ppermute | solution.py:80
  121.6 14.7 %route_cotangent.1 = (bf16[8,256,320]{2,1,0:T(8,128)(2,1)}, bf16[8,320,2048]{2,1,0:T(8,128)(2,1)}) custom-call(s32[2]{0:T(128)} %pad_add_fusion.refs_0_.pos_ref, bf16[2048,2176]{1,0:T(8,128)(2,1)} %all-gather.3.cloned.1.call-done.refs_1_, bf16[128,2176]{1,0:T(8,128)(2,1)} %joins.5.refs_2_.refs_0_), custom_call_target="tpu_custom_call" | custom-call | flops 100000000 | bytes 300000 | tf_op jit(solution)/shard_map/route_cotangent/pallas_call | solution.py:1010
  141.7 9.3 %down_back.1.refs_1_.down_ref = f32[8,320,256]{2,1,0:T(8,128)} custom-call(bf16[8,320,2048]{2,1,0:T(8,128)(2,1)} %get-tuple-element.91.refs_0_.refs_1_, bf16[8,3,2048,256]{3,2,1,0:T(8,128)(2,1)} %refs_3_.1, bf16[128,2176]{1,0:T(8,128)(2,1)} %joins.6.refs_2_.refs_8_), custom_call_target="tpu_custom_call" | custom-call | flops 100000000 | bytes 300000 | tf_op jit(solution)/shard_map/down_back/pallas_call | solution.py:1038
  151.0 3.8 collective-permute-done.28.refs_0_.refs_10_
  159.6 4.6 %collective-permute-done.25.refs_6_ = bf16[128,2176]{1,0:T(8,128)(2,1)S(1)} collective-permute-done((bf16[128,2176]{1,0:T(8,128)(2,1)S(1)}, bf16[128,2176]{1,0:T(8,128)(2,1)S(1)}, u32[]{:S(2)}, u32[]{:S(2)}) %collective-permute-start.25) | collective-permute-done | bytes 557088 | tf_op jit(solution)/shard_map/ppermute | solution.py:80
  164.8 5.7 %collective-permute-done.30.refs_12_ = bf16[128,2176]{1,0:T(8,128)(2,1)} collective-permute-done((bf16[128,2176]{1,0:T(8,128)(2,1)S(1)}, bf16[128,2176]{1,0:T(8,128)(2,1)}, u32[]{:S(2)}, u32[]{:S(2)}) %collective-permute-start.30) | collective-permute-done | bytes 557088 | tf_op jit(solution)/shard_map/ppermute | solution.py:80
  170.5 7.5 %collective-permute-done.32.refs_14_ = bf16[128,2176]{1,0:T(8,128)(2,1)S(1)} collective-permute-done((bf16[128,2176]{1,0:T(8,128)(2,1)}, bf16[128,2176]{1,0:T(8,128)(2,1)S(1)}, u32[]{:S(2)}, u32[]{:S(2)}) %collective-permute-start.32) | collective-permute-done | bytes 557088 | tf_op jit(solution)/shard_map/ppermute | solution.py:80
  180.1 31.6 %run_experts.1 = (bf16[8,320,2048]{2,1,0:T(8,128)(2,1)}, bf16[8,320,256]{2,1,0:T(8,128)(2,1)}, bf16[8,320,256]{2,1,0:T(8,128)(2,1)}, bf16[8,320,256]{2,1,0:T(8,1...) custom-call(s32[2]{0:T(128)} %pad_add_fusion.refs_0_.pos_ref, ...), custom_call_target="tpu_custom_call" | custom-call | flops 5000000000 | bytes 15000000 | tf_op jit(solution)/shard_map/run_experts/pallas_call | solution.py:1138
  212.3 4.0 collective-permute-done.37.refs_1_
  226.0 12.9 %expert_outputs.1.refs_4_ = bf16[8,256,2048]{2,1,0:T(8,128)(2,1)} custom-call(s32[2]{0:T(128)S(1)} %copy-done.33, bf16[8,256,320]{2,1,0:T(8,128)(2,1)S(1)} %copy-done.4, bf16[8,320,256]{2,1,0:T(8,128)(2,1)S(1)} %copy-done.5, bf16[8,3,2048,256]{3,2,1,0:T(8,128)(2,1)} %refs_3_.1, bf16[2,64,2176]{2,1,0:T(8,128)(2,1)} %get-tuple-element.98.refs_4_, ...), custom_call_target="tpu_custom_call" | custom-call | flops 100000000 | bytes 300000 | tf_op jit(solution)/shard_map/expert_outputs/pallas_call | solution.py:1209
  264.6 15.2 %expert_gradients.2 = (f32[8,3,2048,256]{3,2,1,0:T(8,128)}, f32[8,128]{1,0:T(8,128)S(1)}) custom-call(bf16[8,320,2048]{2,1,0:T(8,128)(2,1)} %get-tuple-element.109.refs_0_, bf16[8,320,2048]{2,1,0:T(8,128)(2,1)} %get-tuple-element.91.refs_0_.refs_1_, bf16[8,320,256]{2,1,0:T(8,128)(2,1)S(1)} %copy-done.6, bf16[8,320,256]{2,1,0:T(8,128)(2,1)S(1)} %copy-done.7, ...), custom_call_target="tpu_custom_call" | custom-call | flops 100000000 | bytes 300000 | tf_op jit(solution)/shard_map/expert_gradients/pallas_call | solution.py:1248
  279.8 3.9 collective-permute-done.45.refs_8_
  290.8 15.1 %expert_gradients.3 = (f32[8,3,2048,256]{3,2,1,0:T(8,128)}, f32[8,128]{1,0:T(8,128)S(1)}) custom-call(bf16[8,320,2048]{2,1,0:T(8,128)(2,1)} %get-tuple-element.109.refs_0_, bf16[8,320,2048]{2,1,0:T(8,128)(2,1)} %get-tuple-element.91.refs_0_.refs_1_, bf16[8,320,256]{2,1,0:T(8,128)(2,1)S(1)} %copy-done.6, ...), custom_call_target="tpu_custom_call", output_to_operand_aliasing={{0}: (5, {})} | custom-call | flops 100000000 | bytes 300000 | tf_op jit(solution)/shard_map/expert_gradients/pallas_call | solution.py:1248
  306.5 5.2 %collective-permute-done.48.refs_14_.refs_4_ = bf16[64,2176]{1,0:T(8,128)(2,1)S(1)} collective-permute-done((bf16[64,2176]{1,0:T(8,128)(2,1)S(1)}, bf16[64,2176]{1,0:T(8,128)(2,1)S(1)}, u32[]{:S(2)}, u32[]{:S(2)}) %collective-permute-start.48) | collective-permute-done | bytes 278560 | tf_op jit(solution)/shard_map/ppermute | solution.py:80
  312.5 11.2 %attend_backward.1 = (bf16[256,1536]{1,0:T(8,128)(2,1)}, bf16[64,4224]{1,0:T(8,128)(2,1)}, bf16[64,4224]{1,0:T(8,128)(2,1)}, bf16[64,4224]{1,0:T(8,128)(2,1)}, bf16[64,4224]{1,0:T(8,128)(2,1)}) custom-call(s32[2]{0:T(128)} %pad_add_fusion.refs_0_.pos_ref, bf16[256,2048]{1,0:T(8,128)(2,1)} %refs_1_.10, f32[256,128]{1,0:T(8,128)} %get-tuple-element.179.refs_2_.refs_13_, ...), custom_call_target="tpu_custom_call" | custom-call | flops 100000000 | bytes 300000 | tf_op jit(solution)/shard_map/attend_backward/pallas_call | solution.py:630
  329.3 4.0 projection_gradients.1
  335.0 12.6 %collective-permute-done.50.refs_6_.refs_11_ = bf16[64,4224]{1,0:T(8,128)(2,1)S(1)} collective-permute-done((bf16[64,4224]{1,0:T(8,128)(2,1)}, bf16[64,4224]{1,0:T(8,128)(2,1)S(1)}, u32[]{:S(2)}, u32[]{:S(2)}) %collective-permute-start.50) | collective-permute-done | bytes 540704 | tf_op jit(solution)/shard_map/ppermute | solution.py:80
  347.5 15.8 %collective-permute-done.51.refs_7_.refs_12_ = bf16[64,4224]{1,0:T(8,128)(2,1)S(1)} collective-permute-done((bf16[64,4224]{1,0:T(8,128)(2,1)}, bf16[64,4224]{1,0:T(8,128)(2,1)S(1)}, u32[]{:S(2)}, u32[]{:S(2)}) %collective-permute-start.51) | collective-permute-done | bytes 540704 | tf_op jit(solution)/shard_map/ppermute | solution.py:80
  363.3 3.6 last_rows.1.refs_2_
  367.1 3.5 pair_sums.6
  380.2 14.3 %collective-permute-done.60.refs_3_.new_y = bf16[2,128,1536]{2,1,0:T(8,128)(2,1)S(1)} collective-permute-done((bf16[2,128,1536]{2,1,0:T(8,128)(2,1)S(1)}, bf16[2,128,1536]{2,1,0:T(8,128)(2,1)S(1)}, u32[]{:S(2)}, u32[]{:S(2)}) %collective-permute-start.60) | collective-permute-done | bytes 786464 | tf_op jit(solution)/shard_map/ppermute | solution.py:80
  395.6 3.2 next_sums.7
  405.8 5.1 %collective-permute-done.61.end_x = bf16[128,1536]{1,0:T(8,128)(2,1)S(1)} collective-permute-done((bf16[128,1536]{1,0:T(8,128)(2,1)S(1)}, bf16[128,1536]{1,0:T(8,128)(2,1)S(1)}, u32[]{:S(2)}, u32[]{:S(2)}) %collective-permute-start.61) | collective-permute-done | bytes 393248 | tf_op jit(solution)/shard_map/ppermute | solution.py:80
  417.0 4.0 all-gather.5.cloned.1.call-done.refs_0_
  (300 shorter events, 132.6 us)
Async XLA Ops:
  7.2 114.4 %all-gather.3.cloned.1.call-start = ((), (), s32[]{:S(2)}) async-start(), calls=%async_computation.1 | async-start | bytes 10027008 | tf_op jit(solution)/shard_map/all_gather | solution.py:1343
  20.7 24.9 %collective-permute-start.8 = (bf16[128,2176]{1,0:T(8,128)(2,1)}, bf16[128,2176]{1,0:T(8,128)(2,1)}, u32[]{:S(2)}, u32[]{:S(2)}) collective-permute-start(bf16[128,2176]{1,0:T(8,128)(2,1)} %concatenate.21.refs_12_.refs_24_), channel_id=1, source_target_pairs={{0,8},{4,12},{8,0},{12,4},{16,24},{20,28},{24,16},{28,20},{1,9},{5... | collective-permute-start | bytes 1671176 | tf_op jit(solution)/shard_map/ppermute | solution.py:80
  21.2 24.4 %collective-permute-start.10 = (bf16[128,2176]{1,0:T(8,128)(2,1)}, bf16[128,2176]{1,0:T(8,128)(2,1)}, u32[]{:S(2)}, u32[]{:S(2)}) collective-permute-start(bf16[128,2176]{1,0:T(8,128)(2,1)} %concatenate.21.refs_12_.refs_24_), channel_id=1, source_target_pairs={{0,16},{4,20},{8,24},{12,28},{16,0},{20,4},{24,8},{28,12},{1,17},{... | collective-permute-start | bytes 1671176 | tf_op jit(solution)/shard_map/ppermute | solution.py:80
  33.6 22.5 %collective-permute-start.5 = (bf16[128,2176]{1,0:T(8,128)(2,1)S(1)}, bf16[128,2176]{1,0:T(8,128)(2,1)}, u32[]{:S(2)}, u32[]{:S(2)}) collective-permute-start(bf16[128,2176]{1,0:T(8,128)(2,1)S(1)} %collective-permute-done.3.refs_8_.refs_4_.refs_20_), channel_id=1, source_target_pairs={{0,8},{4,12},{8,0},{12,4},{16,24},{20,28},{24,16},{28,20},{1,9},{5... | collective-permute-start | bytes 1671176 | tf_op jit(solution)/shard_map/ppermute | solution.py:80
  36.3 22.2 %collective-permute-start.4 = (bf16[128,2176]{1,0:T(8,128)(2,1)S(1)}, bf16[128,2176]{1,0:T(8,128)(2,1)S(1)}, u32[]{:S(2)}, u32[]{:S(2)}) collective-permute-start(bf16[128,2176]{1,0:T(8,128)(2,1)S(1)} %collective-permute-done.3.refs_8_.refs_4_.refs_20_), channel_id=1, source_target_pairs={{0,4},{4,0},{8,12},{12,8},{16,20},{20,16},{24,28},{28,24},{1,5},{5... | collective-permute-start | bytes 1671176 | tf_op jit(solution)/shard_map/ppermute | solution.py:80
  62.6 249.1 %reduce-scatter.2.cloned.1.call-start = ((), (), s32[]{:S(2)}) async-start(), calls=%async_computation.2 | async-start | bytes 9437184 | tf_op jit(solution)/shard_map/reduce_scatter | solution.py:1372
  79.4 21.5 %collective-permute-start.15 = (bf16[64,2048]{1,0:T(8,128)(2,1)}, bf16[64,2048]{1,0:T(8,128)(2,1)S(1)}, u32[]{:S(2)}, u32[]{:S(2)}) collective-permute-start(bf16[64,2048]{1,0:T(8,128)(2,1)} %get-tuple-element.85), channel_id=1, source_target_pairs={{0,2},{1,3},{2,0},{3,1},{4,6},{5,7},{6,4},{7,5},{8,10},{9,11},{10,... | collective-permute-start | bytes 786440 | tf_op jit(solution)/shard_map/ppermute | solution.py:80
  109.9 26.4 %collective-permute-start.19 = (bf16[64,2176]{1,0:T(8,128)(2,1)}, bf16[64,2176]{1,0:T(8,128)(2,1)S(1)}, u32[]{:S(2)}, u32[]{:S(2)}) collective-permute-start(bf16[64,2176]{1,0:T(8,128)(2,1)} %get-tuple-element.89.refs_0_.refs_6_), channel_id=1, source_target_pairs={{0,3},{1,2},{2,1},{3,0},{4,7},{5,6},{6,5},{7,4},{8,11},{9,10},{10,... | collective-permute-start | bytes 835592 | tf_op jit(solution)/shard_map/ppermute | solution.py:80
  112.4 24.0 %collective-permute-start.18 = (bf16[64,2176]{1,0:T(8,128)(2,1)}, bf16[64,2176]{1,0:T(8,128)(2,1)S(1)}, u32[]{:S(2)}, u32[]{:S(2)}) collective-permute-start(bf16[64,2176]{1,0:T(8,128)(2,1)} %get-tuple-element.89.refs_0_.refs_6_), channel_id=1, source_target_pairs={{0,2},{1,3},{2,0},{3,1},{4,6},{5,7},{6,4},{7,5},{8,10},{9,11},{10,... | collective-permute-start | bytes 835592 | tf_op jit(solution)/shard_map/ppermute | solution.py:80
  119.9 19.7 %collective-permute-start.23 = (bf16[128,2176]{1,0:T(8,128)(2,1)}, bf16[128,2176]{1,0:T(8,128)(2,1)S(1)}, u32[]{:S(2)}, u32[]{:S(2)}) collective-permute-start(bf16[128,2176]{1,0:T(8,128)(2,1)} %joins.5.refs_2_.refs_0_), channel_id=1, source_target_pairs={{0,16},{4,20},{8,24},{12,28},{16,0},{20,4},{24,8},{28,12},{1,17},{... | collective-permute-start | bytes 1671176 | tf_op jit(solution)/shard_map/ppermute | solution.py:80
  120.1 21.3 %collective-permute-start.21 = (bf16[128,2176]{1,0:T(8,128)(2,1)}, bf16[128,2176]{1,0:T(8,128)(2,1)S(1)}, u32[]{:S(2)}, u32[]{:S(2)}) collective-permute-start(bf16[128,2176]{1,0:T(8,128)(2,1)} %joins.5.refs_2_.refs_0_), channel_id=1, source_target_pairs={{0,8},{4,12},{8,0},{12,4},{16,24},{20,28},{24,16},{28,20},{1,9},{5... | collective-permute-start | bytes 1671176 | tf_op jit(solution)/shard_map/ppermute | solution.py:80
  139.6 24.5 %collective-permute-start.25 = (bf16[128,2176]{1,0:T(8,128)(2,1)S(1)}, bf16[128,2176]{1,0:T(8,128)(2,1)S(1)}, u32[]{:S(2)}, u32[]{:S(2)}) collective-permute-start(bf16[128,2176]{1,0:T(8,128)(2,1)S(1)} %collective-permute-done.23.refs_4_), channel_id=1, source_target_pairs={{0,8},{4,12},{8,0},{12,4},{16,24},{20,28},{24,16},{28,20},{1,9},{5... | collective-permute-start | bytes 1671176 | tf_op jit(solution)/shard_map/ppermute | solution.py:80
  141.2 23.0 %collective-permute-start.24 = (bf16[128,2176]{1,0:T(8,128)(2,1)S(1)}, bf16[128,2176]{1,0:T(8,128)(2,1)}, u32[]{:S(2)}, u32[]{:S(2)}) collective-permute-start(bf16[128,2176]{1,0:T(8,128)(2,1)S(1)} %collective-permute-done.23.refs_4_), channel_id=1, source_target_pairs={{0,4},{4,0},{8,12},{12,8},{16,20},{20,16},{24,28},{28,24},{1,5},{5... | collective-permute-start | bytes 1671176 | tf_op jit(solution)/shard_map/ppermute | solution.py:80
  141.3 23.4 %collective-permute-start.22 = (bf16[128,2176]{1,0:T(8,128)(2,1)S(1)}, bf16[128,2176]{1,0:T(8,128)(2,1)}, u32[]{:S(2)}, u32[]{:S(2)}) collective-permute-start(bf16[128,2176]{1,0:T(8,128)(2,1)S(1)} %collective-permute-done.21.refs_2_), channel_id=1, source_target_pairs={{0,4},{4,0},{8,12},{12,8},{16,20},{20,16},{24,28},{28,24},{1,5},{5... | collective-permute-start | bytes 1671176 | tf_op jit(solution)/shard_map/ppermute | solution.py:80
  219.4 19.6 %collective-permute-start.39 = (bf16[2,64,2176]{2,1,0:T(8,128)(2,1)}, bf16[2,64,2176]{2,1,0:T(8,128)(2,1)}, u32[]{:S(2)}, u32[]{:S(2)}) collective-permute-start(bf16[2,64,2176]{2,1,0:T(8,128)(2,1)} %get-tuple-element.99), channel_id=1, source_target_pairs={{0,16},{4,20},{8,24},{12,28},{16,0},{20,4},{24,8},{28,12},{1,17},{... | collective-permute-start | bytes 1671176 | tf_op jit(solution)/shard_map/ppermute | solution.py:80
  224.1 23.1 %collective-permute-start.36 = (bf16[2,64,2176]{2,1,0:T(8,128)(2,1)}, bf16[2,64,2176]{2,1,0:T(8,128)(2,1)}, u32[]{:S(2)}, u32[]{:S(2)}) collective-permute-start(bf16[2,64,2176]{2,1,0:T(8,128)(2,1)} %get-tuple-element.95), channel_id=1, source_target_pairs={{0,16},{4,20},{8,24},{12,28},{16,0},{20,4},{24,8},{28,12},{1,17},{... | collective-permute-start | bytes 1671176 | tf_op jit(solution)/shard_map/ppermute | solution.py:80
  224.6 24.4 %collective-permute-start.35 = (bf16[2,64,2176]{2,1,0:T(8,128)(2,1)}, bf16[2,64,2176]{2,1,0:T(8,128)(2,1)}, u32[]{:S(2)}, u32[]{:S(2)}) collective-permute-start(bf16[2,64,2176]{2,1,0:T(8,128)(2,1)} %get-tuple-element.94.refs_5_), channel_id=1, source_target_pairs={{0,8},{4,12},{8,0},{12,4},{16,24},{20,28},{24,16},{28,20},{1,9},{5... | collective-permute-start | bytes 1671176 | tf_op jit(solution)/shard_map/ppermute | solution.py:80
  238.9 182.1 %all-gather.5.cloned.1.call-start = ((), (), s32[]{:S(2)}) async-start(), calls=%async_computation.3 | async-start | bytes 2621440 | tf_op jit(solution)/shard_map/all_gather | solution.py:1402
  257.4 22.5 %collective-permute-start.46 = (bf16[64,2176]{1,0:T(8,128)(2,1)S(1)}, bf16[64,2176]{1,0:T(8,128)(2,1)S(1)}, u32[]{:S(2)}, u32[]{:S(2)}) collective-permute-start(bf16[64,2176]{1,0:T(8,128)(2,1)S(1)} %get-tuple-element.108), channel_id=1, source_target_pairs={{0,3},{1,2},{2,1},{3,0},{4,7},{5,6},{6,5},{7,4},{8,11},{9,10},{10,... | collective-permute-start | bytes 835592 | tf_op jit(solution)/shard_map/ppermute | solution.py:80
  260.2 23.5 %collective-permute-start.45 = (bf16[64,2176]{1,0:T(8,128)(2,1)S(1)}, bf16[64,2176]{1,0:T(8,128)(2,1)S(1)}, u32[]{:S(2)}, u32[]{:S(2)}) collective-permute-start(bf16[64,2176]{1,0:T(8,128)(2,1)S(1)} %get-tuple-element.105.refs_6_), channel_id=1, source_target_pairs={{0,2},{1,3},{2,0},{3,1},{4,6},{5,7},{6,4},{7,5},{8,10},{9,11},{10,... | collective-permute-start | bytes 835592 | tf_op jit(solution)/shard_map/ppermute | solution.py:80
  263.7 20.0 %collective-permute-start.44 = (bf16[64,2176]{1,0:T(8,128)(2,1)S(1)}, bf16[64,2176]{1,0:T(8,128)(2,1)S(1)}, u32[]{:S(2)}, u32[]{:S(2)}) collective-permute-start(bf16[64,2176]{1,0:T(8,128)(2,1)S(1)} %get-tuple-element.107), channel_id=1, source_target_pairs={{0,1},{1,0},{2,3},{3,2},{4,5},{5,4},{6,7},{7,6},{8,9},{9,8},{10,11... | collective-permute-start | bytes 835592 | tf_op jit(solution)/shard_map/ppermute | solution.py:80
  286.4 20.1 %collective-permute-start.49 = (bf16[64,2176]{1,0:T(8,128)(2,1)S(1)}, bf16[64,2176]{1,0:T(8,128)(2,1)S(1)}, u32[]{:S(2)}, u32[]{:S(2)}) collective-permute-start(bf16[64,2176]{1,0:T(8,128)(2,1)S(1)} %get-tuple-element.120.refs_6_.refs_12_.refs_2_), channel_id=1, source_target_pairs={{0,3},{1,2},{2,1},{3,0},{4,7},{5,6},{6,5},{7,4},{8,11},{9,10},{10,... | collective-permute-start | bytes 835592 | tf_op jit(solution)/shard_map/ppermute | solution.py:80
  288.9 22.8 %collective-permute-start.48 = (bf16[64,2176]{1,0:T(8,128)(2,1)S(1)}, bf16[64,2176]{1,0:T(8,128)(2,1)S(1)}, u32[]{:S(2)}, u32[]{:S(2)}) collective-permute-start(bf16[64,2176]{1,0:T(8,128)(2,1)S(1)} %get-tuple-element.120.refs_6_.refs_12_.refs_2_), channel_id=1, source_target_pairs={{0,2},{1,3},{2,0},{3,1},{4,6},{5,7},{6,4},{7,5},{8,10},{9,11},{10,... | collective-permute-start | bytes 835592 | tf_op jit(solution)/shard_map/ppermute | solution.py:80
  288.9 22.8 %collective-permute-start.47 = (bf16[64,2176]{1,0:T(8,128)(2,1)S(1)}, bf16[64,2176]{1,0:T(8,128)(2,1)S(1)}, u32[]{:S(2)}, u32[]{:S(2)}) collective-permute-start(bf16[64,2176]{1,0:T(8,128)(2,1)S(1)} %get-tuple-element.120.refs_6_.refs_12_.refs_2_), channel_id=1, source_target_pairs={{0,1},{1,0},{2,3},{3,2},{4,5},{5,4},{6,7},{7,6},{8,9},{9,8},{10,11... | collective-permute-start | bytes 835592 | tf_op jit(solution)/shard_map/ppermute | solution.py:80
  323.7 23.9 %collective-permute-start.50 = (bf16[64,4224]{1,0:T(8,128)(2,1)}, bf16[64,4224]{1,0:T(8,128)(2,1)S(1)}, u32[]{:S(2)}, u32[]{:S(2)}) collective-permute-start(bf16[64,4224]{1,0:T(8,128)(2,1)} %get-tuple-element.124), channel_id=1, source_target_pairs={{0,1},{1,0},{2,3},{3,2},{4,5},{5,4},{6,7},{7,6},{8,9},{9,8},{10,11... | collective-permute-start | bytes 1622024 | tf_op jit(solution)/shard_map/ppermute | solution.py:80
  323.7 39.6 %collective-permute-start.51 = (bf16[64,4224]{1,0:T(8,128)(2,1)}, bf16[64,4224]{1,0:T(8,128)(2,1)S(1)}, u32[]{:S(2)}, u32[]{:S(2)}) collective-permute-start(bf16[64,4224]{1,0:T(8,128)(2,1)} %get-tuple-element.125), channel_id=1, source_target_pairs={{0,2},{1,3},{2,0},{3,1},{4,6},{5,7},{6,4},{7,5},{8,10},{9,11},{10,... | collective-permute-start | bytes 1622024 | tf_op jit(solution)/shard_map/ppermute | solution.py:80
  325.9 37.4 %collective-permute-start.52 = (bf16[64,4224]{1,0:T(8,128)(2,1)}, bf16[64,4224]{1,0:T(8,128)(2,1)S(1)}, u32[]{:S(2)}, u32[]{:S(2)}) collective-permute-start(bf16[64,4224]{1,0:T(8,128)(2,1)} %get-tuple-element.126), channel_id=1, source_target_pairs={{0,3},{1,2},{2,1},{3,0},{4,7},{5,6},{6,5},{7,4},{8,11},{9,10},{10,... | collective-permute-start | bytes 1622024 | tf_op jit(solution)/shard_map/ppermute | solution.py:80
  335.0 32.1 %collective-permute-start.53 = (bf16[4,256,1536]{2,1,0:T(8,128)(2,1)}, bf16[4,256,1536]{2,1,0:T(8,128)(2,1)}, u32[]{:S(2)}, u32[]{:S(2)}) collective-permute-start(bf16[4,256,1536]{2,1,0:T(8,128)(2,1)} %get-tuple-element.131), channel_id=1, source_target_pairs={{0,4},{4,0},{8,12},{12,8},{16,20},{20,16},{24,28},{28,24},{1,5},{5... | collective-permute-start | bytes 9437192 | tf_op jit(solution)/shard_map/ppermute | solution.py:80
  374.2 20.3 %collective-permute-start.60 = (bf16[2,128,1536]{2,1,0:T(8,128)(2,1)S(1)}, bf16[2,128,1536]{2,1,0:T(8,128)(2,1)S(1)}, u32[]{:S(2)}, u32[]{:S(2)}) collective-permute-start(bf16[2,128,1536]{2,1,0:T(8,128)(2,1)S(1)} %get-tuple-element.140), channel_id=1, source_target_pairs={{0,16},{4,20},{8,24},{12,28},{16,0},{20,4},{24,8},{28,12},{1,17},{... | collective-permute-start | bytes 2359304 | tf_op jit(solution)/shard_map/ppermute | solution.py:80
  375.2 20.4 %collective-permute-start.59 = (bf16[2,128,1536]{2,1,0:T(8,128)(2,1)S(1)}, bf16[2,128,1536]{2,1,0:T(8,128)(2,1)S(1)}, u32[]{:S(2)}, u32[]{:S(2)}) collective-permute-start(bf16[2,128,1536]{2,1,0:T(8,128)(2,1)S(1)} %get-tuple-element.132.refs_14_), channel_id=1, source_target_pairs={{0,8},{4,12},{8,0},{12,4},{16,24},{20,28},{24,16},{28,20},{1,9},{5... | collective-permute-start | bytes 2359304 | tf_op jit(solution)/shard_map/ppermute | solution.py:80
  378.5 24.1 %collective-permute-start.55 = (bf16[2,128,640]{2,1,0:T(8,128)(2,1)S(1)}, bf16[2,128,640]{2,1,0:T(8,128)(2,1)S(1)}, u32[]{:S(2)}, u32[]{:S(2)}) collective-permute-start(bf16[2,128,640]{2,1,0:T(8,128)(2,1)S(1)} %get-tuple-element.135), channel_id=1, source_target_pairs={{0,8},{4,12},{8,0},{12,4},{16,24},{20,28},{24,16},{28,20},{1,9},{5... | collective-permute-start | bytes 983048 | tf_op jit(solution)/shard_map/ppermute | solution.py:80
  379.5 23.1 %collective-permute-start.56 = (bf16[2,128,640]{2,1,0:T(8,128)(2,1)S(1)}, bf16[2,128,640]{2,1,0:T(8,128)(2,1)S(1)}, u32[]{:S(2)}, u32[]{:S(2)}) collective-permute-start(bf16[2,128,640]{2,1,0:T(8,128)(2,1)S(1)} %get-tuple-element.136), channel_id=1, source_target_pairs={{0,16},{4,20},{8,24},{12,28},{16,0},{20,4},{24,8},{28,12},{1,17},{... | collective-permute-start | bytes 983048 | tf_op jit(solution)/shard_map/ppermute | solution.py:80
  (100 other events, 816.1 us)
Sparse Core Ops, SparseCore 0:
  62.7 57.0 all-gather.2
  239.0 71.5 reduce-scatter.1
  367.1 53.8 all-gather.4
